TPU v7x, 128 devices: a whole 4x4x4 slice. The times are simulated.
128 devices in a mesh: energy: 8 (over z, core), views: 16 (over y, x).
Axes of the slice: x: 4, y: 4, z: 4, core: 2. Of those that a mesh axis runs over, the one named last changes fastest.
Arguments:
- projector_tiles: float32 [64, 48, 128, 256], P('views'), may hold values from -0.0546875 to 0.0546875
- tile_blocks: int32 [64, 48], P('views'), may hold values from 0 to 255
- ray_counts: int32 [64], P('views'), may hold values from 64 to 128
- sinogram: float32 [64, 8192], P('energy', 'views'), may hold values from -6 to 6
- ray_weights: float32 [64, 8192], P('energy', 'views'), may hold values from 0.25 to 4
- start_volume: float32 [64, 65536], P('energy', 'views'), may hold values from -6 to 6
- split_target: float32 [16, 64, 4096], P('views', None, 'energy'), may hold values from -6 to 6
- scaled_dual: float32 [16, 64, 4096], P('views', None, 'energy'), may hold values from -3 to 3
Outputs:
- new_volume: float32 [64, 65536], P('energy', 'views')
- new_split: float32 [16, 64, 4096], P('views', None, 'energy')
- new_dual: float32 [16, 64, 4096], P('views', None, 'energy')
Inputs may be any that keep to these rules, and one draw needn't show every extreme that they name: `tile_blocks`: block indices may repeat within a ray block. `ray_counts`: rays of a block at or past its count are padding.
All inputs are finite; a program needn't handle non-finite values.
Results may differ from a plain program's by a relative error of at most 0.00022.
Values sent between devices are 32-bit elements; how exact they have to be, the bound alone decides.
A program may use at most 128 MiB of HBM per device.

v0:
```python
import jax
import jax.numpy as jnp
from jax import lax
from jax.sharding import PartitionSpec as P

PV = 64
ITERS = 3


PENALTY = 1.0
SHRINK = 16.0
exact_mode = lax.Precision.HIGHEST


def forward(gathered, projector_tiles, tile_blocks):
    channel_count = gathered.shape[0]
    block_voxels = projector_tiles.shape[3]
    block_grid = gathered.reshape(channel_count, -1, block_voxels)
    columns = block_grid[:, tile_blocks]
    projected = jnp.einsum("crtv,rtkv->crk", columns, projector_tiles, precision=exact_mode)
    return projected.reshape(channel_count, -1)


def backward(weighted, projector_tiles, tile_blocks, voxel_count):
    channel_count = weighted.shape[0]
    ray_blocks, per_block, ray_length, block_voxels = projector_tiles.shape
    ray_parts = weighted.reshape(channel_count, ray_blocks, ray_length)
    spread_rays = jnp.einsum("crk,rtkv->crtv", ray_parts, projector_tiles, precision=exact_mode)
    block_grid = jnp.zeros((channel_count, voxel_count // block_voxels, block_voxels), jnp.float32)
    block_grid = block_grid.at[:, tile_blocks.reshape(-1)].add(
        spread_rays.reshape(channel_count, ray_blocks * per_block, block_voxels)
    )
    return block_grid.reshape(channel_count, voxel_count)


def shrink_patches(merged):
    leading, channel_count, segment_len = merged.shape
    blocks = merged.reshape(channel_count, segment_len // PV, PV)
    gram_matrix = jnp.einsum("cpv,dpv->pcd", blocks, blocks, precision=exact_mode)
    shifted = gram_matrix + SHRINK * jnp.eye(channel_count, dtype=jnp.float32)
    factor = jnp.linalg.cholesky(shifted)
    right_side = jnp.transpose(blocks, (1, 0, 2))
    solved = jax.scipy.linalg.cho_solve((factor, True), right_side)
    shrunk = right_side - SHRINK * solved
    return jnp.transpose(shrunk, (1, 0, 2)).reshape(leading, channel_count, segment_len)


def local(
    projector_tiles,
    tile_blocks,
    ray_counts,
    sinogram,
    ray_weights,
    start_volume,
    split_target,
    scaled_dual,
):
    ray_length = projector_tiles.shape[2]
    live_rays = (
        lax.broadcasted_iota(jnp.int32, (ray_counts.shape[0], ray_length), 1) < ray_counts[:, None]
    ).astype(jnp.float32)
    ray_scale = ray_weights * live_rays.reshape(1, -1)
    target_shard = lax.all_to_all(
        split_target - scaled_dual, "energy", split_axis=1, concat_axis=2, tiled=True
    )[0]
    segment = target_shard.shape[1]
    voxel_count = segment * lax.axis_size("views")
    volume_now, target = (start_volume, target_shard)

    def normal_map(vector, measured, anchor):
        gathered = lax.all_gather(vector, "views", axis=1, tiled=True)
        weighted = ray_scale * (measured - forward(gathered, projector_tiles, tile_blocks))
        partial_sum = backward(weighted, projector_tiles, tile_blocks, voxel_count)
        summed = lax.psum_scatter(partial_sum, "views", scatter_dimension=1, tiled=True)
        return summed + PENALTY * (anchor - vector)

    residual = normal_map(volume_now, sinogram, target)

    def norm_total(vector):
        return lax.psum(jnp.sum(jnp.square(vector), axis=1), "views")

    direction = residual
    norm_now = norm_total(residual)
    for iteration in range(ITERS):
        mapped = -normal_map(direction, 0.0, 0.0)
        curvature = lax.psum(jnp.sum(direction * mapped, axis=1), "views")
        step_size = (norm_now / curvature)[:, None]
        volume_now = volume_now + step_size * direction
        if iteration + 1 < ITERS:
            residual = residual - step_size * mapped
            norm_next = norm_total(residual)
            direction = residual + (norm_next / norm_now)[:, None] * direction
            norm_now = norm_next
    volume_patch = lax.all_to_all(
        volume_now[None], "energy", split_axis=2, concat_axis=1, tiled=True
    )
    new_split = shrink_patches(volume_patch + scaled_dual)
    new_dual = scaled_dual + volume_patch - new_split
    return (volume_now, new_split, new_dual)


def solution(mesh):
    placed = (
        P("views", None, None, None),
        P("views", None),
        P("views"),
        P("energy", "views"),
        P("energy", "views"),
        P("energy", "views"),
        P("views", None, "energy"),
        P("views", None, "energy"),
    )
    return jax.shard_map(
        local,
        mesh=mesh,
        in_specs=placed,
        out_specs=(P("energy", "views"), P("views", None, "energy"), P("views", None, "energy")),
        check_vma=False,
    )
```

profile of v0, /device:TPU:1, one launch (start us, length us, event | category | flops | bytes accessed | tf_op | source)
XLA Modules:
  0.0 1047.2 jit_solution(1356048474511867620)
XLA Ops:
  7.2 0.7 all-gather.5.cloned.1.call-update
  8.0 0.8 reshape.153
  8.7 0.7 compare_select_fusion.1
  9.5 0.7 convert_bitcast_fusion
  10.2 47.1 %all-gather.5.cloned.1.call-done = f32[8,65536]{1,0:T(8,128)} async-done(((f32[8,4096]{1,0:T(8,128)}), f32[8,65536]{1,0:T(8,128)}) %all-gather.5.cloned.1.call-update) | async-done | bytes 2097168 | tf_op jit(solution)/shard_map/all_gather | solution.py:71
  57.4 2.3 gather_fusion
  59.7 24.1 %fusion.16 = f32[8,4,128,1]{2,0,3,1:T(8,128)S(1)} fusion(f32[8,512]{1,0:T(8,128)S(1)} %copy-done.14, f32[8,4,48,256]{3,0,2,1:T(8,128)S(1)} %bitcast.197, f32[4,48,128,256]{3,2,1,0:T(8,128)} %param.8, f32[8,512]{1,0:T(8,128)S(1)} %copy-done.12, f32[512]{0:T(512)S(1)} %convert_bitcast_fusion), kind=kOutput, calls=%fused_computation.29 | convolution fusion | flops 603992064 | bytes 26789888 | tf_op jit(solution)/shard_map/crtv,rtkv->crk/dot_general | solution.py:20
  83.8 12.9 %fusion.26 = f32[4,8,48,256]{3,1,2,0:T(8,128)} fusion(f32[8,4,128,1]{2,0,3,1:T(8,128)S(1)} %fusion.16, f32[4,48,128,256]{3,2,1,0:T(8,128)S(1)} %copy-done), kind=kOutput, calls=%fused_computation.67 | convolution fusion | flops 603979776 | bytes 26755072 | tf_op jit(solution)/shard_map/crk,rtkv->crtv/dot_general | solution.py:28
  96.9 15.5 %scatter_fusion = f32[8,256,256]{2,0,1:T(8,128)S(1)} fusion(f32[8,256,256]{2,0,1:T(8,128)S(1)} %broadcast.144.clone, s32[192]{0:T(256)S(1)} %bitcast.206, f32[192,8,256]{2,1,0:T(8,128)} %bitcast.191), kind=kCustom, calls=%fused_computation.4 | custom fusion | flops 393216 | bytes 4719360 | tf_op jit(solution)/shard_map/scatter-add | solution.py:30
  112.5 1.3 copy-done.2
  114.0 11.0 %all_to_all.33 = f32[1,64,512]{2,0,1:T(1,128)S(1)} all-to-all(f32[1,64,512]{2,0,1:T(1,128)S(1)} %copy.60), channel_id=1, replica_groups=mesh['energy'=8,'views'=16] {'energy'}, dimensions={1} | all-to-all | bytes 262144 | tf_op jit(solution)/shard_map/all_to_all | solution.py:63
  125.0 61.7 %reduce-scatter.5.cloned.1.call-done = f32[8,4096]{1,0:T(8,128)} async-done(((f32[8,65536]{1,0:T(8,128)}), f32[8,4096]{1,0:T(8,128)}) %reduce-scatter.5.cloned.1.call-update) | async-done | bytes 131088 | tf_op jit(solution)/shard_map/reduce_scatter | solution.py:74
  186.7 1.6 subtract_add_fusion
  188.3 0.3 reduce-scatter.7.cloned.1.call-start
  188.7 46.0 %all-gather.7.cloned.1.call-done = f32[8,65536]{1,0:T(8,128)} async-done(((f32[8,4096]{1,0:T(8,128)}), f32[8,65536]{1,0:T(8,128)}) %all-gather.7.cloned.1.call-update) | async-done | bytes 2097168 | tf_op jit(solution)/shard_map/all_gather | solution.py:71
  234.7 2.3 gather_fusion.1
  237.0 22.7 %fusion.13 = f32[8,4,128,1]{2,0,3,1:T(8,128)S(1)} fusion(f32[8,4,48,256]{3,0,2,1:T(8,128)S(1)} %bitcast.195, f32[4,48,128,256]{3,2,1,0:T(8,128)} %param.8, f32[8,512]{1,0:T(8,128)S(1)} %copy-done.12, f32[512]{0:T(512)S(1)} %convert_bitcast_fusion), kind=kOutput, calls=%fused_computation.25 | convolution fusion | flops 603992064 | bytes 26773504 | tf_op jit(solution)/shard_map/crtv,rtkv->crk/dot_general | solution.py:20
  259.6 15.8 %fusion.27 = f32[4,8,48,256]{3,1,2,0:T(8,128)} fusion(f32[8,4,128,1]{2,0,3,1:T(8,128)S(1)} %fusion.13, f32[4,48,128,256]{3,2,1,0:T(8,128)} %param.8), kind=kOutput, calls=%fused_computation.68 | convolution fusion | flops 603979776 | bytes 26755072 | tf_op jit(solution)/shard_map/crk,rtkv->crtv/dot_general | solution.py:28
  275.6 15.5 %scatter_fusion.1 = f32[8,256,256]{2,0,1:T(8,128)S(1)} fusion(f32[8,256,256]{2,0,1:T(8,128)S(1)} %broadcast.144.clone.1, s32[192]{0:T(256)S(1)} %bitcast.207, f32[192,8,256]{2,1,0:T(8,128)} %bitcast.192), kind=kCustom, calls=%fused_computation.5 | custom fusion | flops 393216 | bytes 4719360 | tf_op jit(solution)/shard_map/scatter-add | solution.py:30
  291.1 1.3 copy-done.3
  292.5 72.9 %reduce-scatter.7.cloned.1.call-done = f32[8,4096]{1,0:T(8,128)} async-done(((f32[8,65536]{1,0:T(8,128)}), f32[8,4096]{1,0:T(8,128)}) %reduce-scatter.7.cloned.1.call-update) | async-done | bytes 131088 | tf_op jit(solution)/shard_map/reduce_scatter | solution.py:74
  365.4 1.1 multiply_reduce_fusion.4
  366.5 30.9 %all-reduce = (f32[8]{0:T(128)S(1)}, f32[8]{0:T(128)S(1)}) all-reduce(f32[8]{0:T(128)S(1)} %get-tuple-element.7, f32[8]{0:T(128)S(1)} %get-tuple-element.6), channel_id=1, replica_groups=mesh['energy'=8,'views'=16] {'views'}, use_global_device_ids=true, to_apply=%region_3.0 | all-reduce | flops 16 | bytes 128 | tf_op jit(solution)/shard_map/psum | solution.py:80
  397.4 1.1 multiply_reduce_fusion.3
  398.5 28.5 %psum.44 = f32[8]{0:T(128)S(1)} all-reduce(f32[8]{0:T(128)S(1)} %get-tuple-element.10), channel_id=1, replica_groups=mesh['energy'=8,'views'=16] {'views'}, use_global_device_ids=true, to_apply=%region_9.0 | all-reduce | flops 8 | bytes 64 | tf_op jit(solution)/shard_map/psum | solution.py:80
  427.0 0.7 multiply_add_fusion.2
  427.8 0.6 reduce-scatter.9.cloned.1.call-start
  428.4 57.2 %all-gather.9.cloned.1.call-done = f32[8,65536]{1,0:T(8,128)} async-done(((f32[8,4096]{1,0:T(8,128)}), f32[8,65536]{1,0:T(8,128)}) %all-gather.9.cloned.1.call-update) | async-done | bytes 2097168 | tf_op jit(solution)/shard_map/all_gather | solution.py:71
  485.6 2.3 gather_fusion.2
  487.9 22.7 %fusion.9 = f32[8,4,128,1]{2,0,3,1:T(8,128)S(1)} fusion(f32[8,4,48,256]{3,0,2,1:T(8,128)S(1)} %bitcast.196, f32[4,48,128,256]{3,2,1,0:T(8,128)} %param.8, f32[8,512]{1,0:T(8,128)S(1)} %copy-done.12, f32[512]{0:T(512)S(1)} %convert_bitcast_fusion), kind=kOutput, calls=%fused_computation.20 | convolution fusion | flops 603992064 | bytes 26773504 | tf_op jit(solution)/shard_map/crtv,rtkv->crk/dot_general | solution.py:20
  510.6 15.8 %fusion.28 = f32[4,8,48,256]{3,1,2,0:T(8,128)} fusion(f32[8,4,128,1]{2,0,3,1:T(8,128)S(1)} %fusion.9, f32[4,48,128,256]{3,2,1,0:T(8,128)} %param.8), kind=kOutput, calls=%fused_computation.69 | convolution fusion | flops 603979776 | bytes 26755072 | tf_op jit(solution)/shard_map/crk,rtkv->crtv/dot_general | solution.py:28
  526.5 15.5 %scatter_fusion.2 = f32[8,256,256]{2,0,1:T(8,128)S(1)} fusion(f32[8,256,256]{2,0,1:T(8,128)S(1)} %broadcast.144.clone.2, s32[192]{0:T(256)S(1)} %bitcast.208, f32[192,8,256]{2,1,0:T(8,128)} %bitcast.193), kind=kCustom, calls=%fused_computation.6 | custom fusion | flops 393216 | bytes 4719360 | tf_op jit(solution)/shard_map/scatter-add | solution.py:30
  542.0 1.3 copy-done.4
  543.4 72.9 %reduce-scatter.9.cloned.1.call-done = f32[8,4096]{1,0:T(8,128)} async-done(((f32[8,65536]{1,0:T(8,128)}), f32[8,4096]{1,0:T(8,128)}) %reduce-scatter.9.cloned.1.call-update) | async-done | bytes 131088 | tf_op jit(solution)/shard_map/reduce_scatter | solution.py:74
  616.3 1.1 multiply_reduce_fusion.2
  617.3 30.9 %psum.45 = f32[8]{0:T(128)S(1)} all-reduce(f32[8]{0:T(128)S(1)} %multiply_reduce_fusion.2), channel_id=1, replica_groups=mesh['energy'=8,'views'=16] {'views'}, use_global_device_ids=true, to_apply=%region_13.0 | all-reduce | flops 8 | bytes 64 | tf_op jit(solution)/shard_map/psum | solution.py:86
  648.2 1.1 multiply_reduce_fusion.1
  649.4 28.5 %psum.46 = f32[8]{0:T(128)S(1)} all-reduce(f32[8]{0:T(128)S(1)} %multiply_reduce_fusion.1), channel_id=1, replica_groups=mesh['energy'=8,'views'=16] {'views'}, use_global_device_ids=true, to_apply=%region_15.0 | all-reduce | flops 8 | bytes 64 | tf_op jit(solution)/shard_map/psum | solution.py:80
  677.9 1.7 multiply_add_fusion.1
  679.5 0.2 reduce-scatter.11.cloned.1.call-start
  679.8 57.6 %all-gather.11.cloned.1.call-done = f32[8,65536]{1,0:T(8,128)} async-done(((f32[8,4096]{1,0:T(8,128)}), f32[8,65536]{1,0:T(8,128)}) %all-gather.11.cloned.1.call-update) | async-done | bytes 2097168 | tf_op jit(solution)/shard_map/all_gather | solution.py:71
  737.4 2.3 gather_fusion.3
  739.7 22.7 %fusion.5 = f32[8,4,128,1]{2,0,3,1:T(8,128)S(1)} fusion(f32[8,4,48,256]{3,0,2,1:T(8,128)S(1)} %bitcast.194, f32[4,48,128,256]{3,2,1,0:T(8,128)} %param.8, f32[8,512]{1,0:T(8,128)S(1)} %copy-done.12, f32[512]{0:T(512)S(1)} %convert_bitcast_fusion), kind=kOutput, calls=%fused_computation.15 | convolution fusion | flops 603992064 | bytes 26773504 | tf_op jit(solution)/shard_map/crtv,rtkv->crk/dot_general | solution.py:20
  762.4 15.8 %fusion.29 = f32[4,8,48,256]{3,1,2,0:T(8,128)} fusion(f32[8,4,128,1]{2,0,3,1:T(8,128)S(1)} %fusion.5, f32[4,48,128,256]{3,2,1,0:T(8,128)} %param.8), kind=kOutput, calls=%fused_computation.70 | convolution fusion | flops 603979776 | bytes 26755072 | tf_op jit(solution)/shard_map/crk,rtkv->crtv/dot_general | solution.py:28
  778.3 15.5 %scatter_fusion.3 = f32[8,256,256]{2,0,1:T(8,128)S(1)} fusion(f32[8,256,256]{2,0,1:T(8,128)S(1)} %broadcast.144, s32[192]{0:T(256)S(1)} %bitcast.209, f32[192,8,256]{2,1,0:T(8,128)} %bitcast.190), kind=kCustom, calls=%fused_computation.7 | custom fusion | flops 393216 | bytes 4719360 | tf_op jit(solution)/shard_map/scatter-add | solution.py:30
  793.8 1.3 copy-done.1
  795.1 73.0 %reduce-scatter.11.cloned.1.call-done = f32[8,4096]{1,0:T(8,128)} async-done(((f32[8,65536]{1,0:T(8,128)}), f32[8,4096]{1,0:T(8,128)}) %reduce-scatter.11.cloned.1.call-update) | async-done | bytes 131088 | tf_op jit(solution)/shard_map/reduce_scatter | solution.py:74
  868.1 1.1 multiply_reduce_fusion
  869.2 31.1 %psum.47 = f32[8]{0:T(128)S(1)} all-reduce(f32[8]{0:T(128)S(1)} %multiply_reduce_fusion), channel_id=1, replica_groups=mesh['energy'=8,'views'=16] {'views'}, use_global_device_ids=true, to_apply=%region_19.0 | all-reduce | flops 8 | bytes 64 | tf_op jit(solution)/shard_map/psum | solution.py:86
  900.4 2.5 copy.62
  902.9 0.5 broadcast.181
  903.4 19.4 %reduce.6 = f32[4096,8]{1,0:T(8,128)} reduce(f32[4096,1,8]{2,1,0:T(1,128)S(1)} %bitcast.188, f32[]{:T(128)} %broadcast.181), dimensions={1}, to_apply=%bitcast.165.reduce_sub_computation | reduce | bytes 262148
  922.8 3.3 reshape.254
  926.1 14.3 %all-to-all-start.1 = ((f32[8,1,4096]{2,1,0:T(1,128)}), f32[8,1,4096]{2,1,0:T(1,128)S(1)}, u32[]{:S(2)}, u32[]{:S(2)}) async-start(f32[8,1,4096]{2,1,0:T(1,128)} %reshape.254), calls=%async_computation.5 | async-start | bytes 262144 | tf_op jit(solution)/shard_map/all_to_all | solution.py:94
  940.4 5.2 all-to-all-done.1
  945.6 1.0 reduce.7
  946.6 3.5 reshape.255
  950.1 0.6 copy.63
  950.8 0.5 fusion.23
  951.5 46.9 %custom-call.11 = f32[8,64,64]{2,1,0:T(8,128)S(1)} custom-call(f32[8,64,64]{2,1,0:T(8,128)S(1)} %fusion.21), custom_call_target="Cholesky" | custom-call | tf_op jit(solution)/shard_map/jit(cholesky)/cholesky | solution.py:41
  998.7 39.3 %custom-call.12 = f32[8,1,64,64]{2,3,1,0:T(8,128)S(1)} custom-call(f32[8,1,64,64]{3,2,1,0:T(8,128)S(1)} %select_bitcast_fusion), custom_call_target="InvertDiagBlocksLowerTriangular" | custom-call | tf_op jit(solution)/shard_map/jit(_cho_solve)/vmap()/triangular_solve | solution.py:43
  1038.0 0.6 fusion.18
  1038.7 0.4 fusion.1
  1039.4 0.7 sub.76
  (66 shorter events, 2.2 us)
Async XLA Ops:
  7.2 52.5 %copy-start.14 = (f32[8,512]{1,0:T(8,128)S(1)}, f32[8,512]{1,0:T(8,128)}, u32[]{:S(2)}) copy-start(f32[8,512]{1,0:T(8,128)} %param.11) | copy-start | bytes 49156
  7.2 52.5 %copy-start.12 = (f32[8,512]{1,0:T(8,128)S(1)}, f32[8,512]{1,0:T(8,128)}, u32[]{:S(2)}) copy-start(f32[8,512]{1,0:T(8,128)} %param.12) | copy-start | bytes 49156
  7.2 50.2 %all-gather.5.cloned.1.call-start = ((), (), s32[]{:S(2)}) async-start(), calls=%async_computation.6 | async-start | bytes 2228224 | tf_op jit(solution)/shard_map/all_gather | solution.py:71
  7.9 178.8 %reduce-scatter.5.cloned.1.call-start = ((), (), s32[]{:S(2)}) async-start(), calls=%async_computation.7 | async-start | bytes 2228224 | tf_op jit(solution)/shard_map/reduce_scatter | solution.py:74
  59.7 24.2 %copy-start = (f32[4,48,128,256]{3,2,1,0:T(8,128)S(1)}, f32[4,48,128,256]{3,2,1,0:T(8,128)}, u32[]{:S(2)}) copy-start(f32[4,48,128,256]{3,2,1,0:T(8,128)} %param.8) | copy-start | bytes 75497472
  112.4 1.4 copy-start.2
  112.4 1.4 copy-start.9
  112.4 1.4 copy-start.13
  112.5 74.3 %copy-start.8 = (f32[8,4096]{1,0:T(8,128)S(1)}, f32[8,4096]{1,0:T(8,128)}, u32[]{:S(2)}) copy-start(f32[8,4096]{1,0:T(8,128)} %param.13) | copy-start | bytes 393220
  113.8 120.9 %all-gather.7.cloned.1.call-start = ((), (), s32[]{:S(2)}) async-start(), calls=%async_computation.8 | async-start | bytes 2228224 | tf_op jit(solution)/shard_map/all_gather | solution.py:71
  188.3 177.1 %reduce-scatter.7.cloned.1.call-start = ((), (), s32[]{:S(2)}) async-start(), calls=%async_computation.9 | async-start | bytes 2228224 | tf_op jit(solution)/shard_map/reduce_scatter | solution.py:74
  291.0 1.4 copy-start.3
  291.1 74.3 %copy-start.5 = (f32[8,4096]{1,0:T(8,128)S(1)}, f32[8,4096]{1,0:T(8,128)}, u32[]{:S(2)}) copy-start(f32[8,4096]{1,0:T(8,128)} %subtract_add_fusion) | copy-start | bytes 393220
  292.4 193.2 %all-gather.9.cloned.1.call-start = ((), (), s32[]{:S(2)}) async-start(), calls=%async_computation.10 | async-start | bytes 2228224 | tf_op jit(solution)/shard_map/all_gather | solution.py:71
  427.8 188.5 %reduce-scatter.9.cloned.1.call-start = ((), (), s32[]{:S(2)}) async-start(), calls=%async_computation.11 | async-start | bytes 2228224 | tf_op jit(solution)/shard_map/reduce_scatter | solution.py:74
  542.0 1.4 copy-start.4
  542.0 74.3 %copy-start.6 = (f32[8,4096]{1,0:T(8,128)S(1)}, f32[8,4096]{1,0:T(8,128)}, u32[]{:S(2)}) copy-start(f32[8,4096]{1,0:T(8,128)} %multiply_add_fusion.2) | copy-start | bytes 393220
  543.4 194.0 %all-gather.11.cloned.1.call-start = ((), (), s32[]{:S(2)}) async-start(), calls=%async_computation.12 | async-start | bytes 2228224 | tf_op jit(solution)/shard_map/all_gather | solution.py:71
  679.5 188.6 %reduce-scatter.11.cloned.1.call-start = ((), (), s32[]{:S(2)}) async-start(), calls=%async_computation.13 | async-start | bytes 2228224 | tf_op jit(solution)/shard_map/reduce_scatter | solution.py:74
  793.8 1.4 copy-start.1
  793.8 74.3 %copy-start.7 = (f32[8,4096]{1,0:T(8,128)S(1)}, f32[8,4096]{1,0:T(8,128)}, u32[]{:S(2)}) copy-start(f32[8,4096]{1,0:T(8,128)} %multiply_add_fusion.1) | copy-start | bytes 393220
  900.4 22.4 %copy-start.11 = (f32[8,4096]{1,0:T(8,128)}, f32[8,4096]{1,0:T(8,128)S(1)}, u32[]{:S(2)}) copy-start(f32[8,4096]{1,0:T(8,128)S(1)} %multiply_add_fusion) | copy-start | bytes 393220
  926.1 19.5 %all-to-all-start.1 = ((f32[8,1,4096]{2,1,0:T(1,128)}), f32[8,1,4096]{2,1,0:T(1,128)S(1)}, u32[]{:S(2)}, u32[]{:S(2)}) async-start(f32[8,1,4096]{2,1,0:T(1,128)} %reshape.254), calls=%async_computation.5 | async-start | bytes 262144 | tf_op jit(solution)/shard_map/all_to_all | solution.py:94
  1039.4 0.7 copy-start.10
Sparse Core Ops, SparseCore 0:
  10.2 47.1 all-gather.4
  113.9 72.7 reduce-scatter.4
  189.7 44.9 all-gather.6
  292.5 72.8 reduce-scatter.6
  427.9 57.6 all-gather.8
  543.5 72.7 reduce-scatter.8
  679.7 57.6 all-gather.10
  795.3 72.8 reduce-scatter.10
where the time goes:
time: 1060 us; the launch traced here: 1050 us
  waiting for transfers between devices  494 us (47%)
  other arithmetic  181 us (17%)
  blocking collectives  161 us (15%)
  matrix products  154 us (15%)
  local copies, waits for them, and re-layouts  27 us (3%)
  starting transfers between devices  15.6 us (1%)
  between operations  14.8 us (1%)
    reduce_scatter x4, waiting for transfers between devices, normal_map(): lax.psum_scatter(partial_sum, 'views', scatter_dimension=1, tiled=True)  280 us
    all_gather x4, waiting for transfers between devices, normal_map(): gathered = lax.all_gather(vector, 'views', axis=1, tiled=True)  208 us
    dot_general x4, matrix products, forward(): jnp.einsum('crtv,rtkv->crk', columns, projector_tiles, precision=exact_mode)  92.2 us
    psum x3, blocking collectives, norm_total(): return lax.psum(jnp.sum(jnp.square(vector), axis=1), 'views')  87.9 us
    psum x2, blocking collectives, local(): curvature = lax.psum(jnp.sum(direction * mapped, axis=1), 'views')  62 us
    scatter-add x4, other arithmetic, backward(): block_grid.at[:, tile_blocks.reshape(-1)]  61.9 us
    dot_general x4, matrix products, backward(): jnp.einsum('crk,rtkv->crtv', ray_parts, projector_tiles, precision=exact_...  60.3 us
    another operation x4, other arithmetic, shrink_patches(): factor = jnp.linalg.cholesky(shifted)  47.1 us
  transfers between devices with their start and end apart: 9, of which 9 were waited for; matrix products, arithmetic and copies ran while one was open for 0% of the time, Pallas kernels for 0%

commit v1 on v0

v1 whole, which is shorter than its diff:
```python
import functools

import jax
import jax.numpy as jnp
from jax import lax
from jax.experimental import pallas as pl
from jax.experimental.pallas import tpu as pltpu
from jax.sharding import PartitionSpec as P

PENALTY = 1.0
SHRINK = 16.0
F32 = jnp.float32
BF16 = jnp.bfloat16
NSTAGE = 4
CH = 8


def split2(v):
    hi = v.astype(BF16)
    lo = (v - hi.astype(F32)).astype(BF16)
    return hi, lo


def lane_total(v):
    return jnp.broadcast_to(jnp.sum(v, axis=1, keepdims=True), v.shape)


def main_kernel(
    idx, counts, tiles, sino, wts, x0, split, dual,
    vol_out, mb_out,
    W, stage,
    V00, V01, V10, V11, V20, V21, V30, V31,
    F, RB1, RB2, R, X, D, T, TP, MB, Pq, Q, WL, AS, AS2, AR,
    dsem, ag_s, ag_r, rs_s, rs_r, ar_s, ar_r, en_s, en_r,
):
    V = ((V00, V01), (V10, V11), (V20, V21), (V30, V31))
    e = lax.axis_index("energy")
    a = lax.axis_index("views")
    y, x = a // 4, a % 4

    def at_views(g, p, s):
        p, s = lax.rem(p + 4, 4), lax.rem(s + 4, 4)
        return {"views": s * 4 + p if g == 0 else p * 4 + s}

    coord = ((x, y), (y, x))

    barrier = pltpu.get_barrier_semaphore()
    for o in (1, 2, 3):
        pl.semaphore_signal(barrier, inc=1, device_id=at_views(0, x + o, y), device_id_type=pl.DeviceIdType.MESH)
        pl.semaphore_signal(barrier, inc=1, device_id=at_views(0, x, y + o), device_id_type=pl.DeviceIdType.MESH)
    for o in range(1, 8):
        pl.semaphore_signal(barrier, inc=1, device_id={"energy": lax.rem(e + o, 8)}, device_id_type=pl.DeviceIdType.MESH)
    pl.semaphore_wait(barrier, 13)

    def tile_copy(c, slot):
        return pltpu.make_async_copy(
            tiles.at[c // 6, pl.ds((c % 6) * CH, CH)], stage.at[slot], dsem.at[slot]
        )

    for c in range(NSTAGE):
        tile_copy(c, c).start()

    def ag(rd, h, g, k):
        p, s = coord[g]
        base = g * 128
        own = base + (s * 4 + p) * 8

        def chunk(pp):
            return base + (s * 4 + lax.rem(pp + 4, 4)) * 8

        def line(ss):
            return base + lax.rem(ss + 4, 4) * 32

        src, size, dev = {
            0: (own, 8, (p + 1, s)),
            1: (own, 8, (p - 1, s)),
            2: (chunk(p - 1), 4, (p + 1, s)),
            3: (chunk(p + 1) + 4, 4, (p - 1, s)),
            4: (line(s), 32, (p, s + 1)),
            5: (line(s), 32, (p, s - 1)),
            6: (line(s - 1), 16, (p, s + 1)),
            7: (line(s + 1) + 16, 16, (p, s - 1)),
        }[k]
        ref = V[rd][h].at[pl.ds(src, size)]
        return pltpu.make_async_remote_copy(
            src_ref=ref, dst_ref=ref,
            send_sem=ag_s.at[rd, h, g, k], recv_sem=ag_r.at[rd, h, g, k],
            device_id=at_views(g, *dev), device_id_type=pl.DeviceIdType.MESH,
        )

    def ag_step(rd, h, n):
        for g in (0, 1):
            if n > 0:
                ag(rd, h, g, 2 * n - 2).wait_recv()
                ag(rd, h, g, 2 * n - 1).wait_recv()
            if n < 4:
                ag(rd, h, g, 2 * n).start()
                ag(rd, h, g, 2 * n + 1).start()

    def ag_sent(rd):
        for h in (0, 1):
            for g in (0, 1):
                for k in range(8):
                    ag(rd, h, g, k).wait_send()

    def rs(rd, h, g, k):
        p, s = coord[g]
        base = g * 128
        kk = k % 6
        if k < 6:
            half = 16

            def row(o):
                return base + lax.rem(s + o + 4, 4) * 32

            def dev(o):
                return at_views(g, p, s + o)

            land = RB1.at[rd, h, g, kk]
        else:
            half = 4

            def row(o):
                return base + (s * 4 + lax.rem(p + o + 4, 4)) * 8

            def dev(o):
                return at_views(g, p + o, s)

            land = RB2.at[rd, h, g, kk]
        src, to = (
            (row(2), -1),
            (row(2) + half, 1),
            (row(-1) + half, -1),
            (row(1), 1),
            (row(-1), -1),
            (row(1) + half, 1),
        )[kk]
        return pltpu.make_async_remote_copy(
            src_ref=F.at[h, pl.ds(src, half)], dst_ref=land,
            send_sem=rs_s.at[rd, h, g, k], recv_sem=rs_r.at[rd, h, g, k],
            device_id=dev(to), device_id_type=pl.DeviceIdType.MESH,
        )

    def rs_step(rd, h, n):
        for g in (0, 1):
            p, s = coord[g]
            base = g * 128
            if n < 2 or n == 2:
                half, RB, k0 = 16, RB1, 0

                def row(o):
                    return base + lax.rem(s + o + 4, 4) * 32
            else:
                half, RB, k0 = 4, RB2, 6

                def row(o):
                    return base + (s * 4 + lax.rem(p + o + 4, 4)) * 8
            if n in (1, 3):
                rs(rd, h, g, k0).wait_recv()
                first = pl.ds(row(-1), half)
                F[h, first] = F[h, first] + RB[rd, h, g, 0]
                rs(rd, h, g, k0 + 4).start()
                rs(rd, h, g, k0 + 1).wait_recv()
                second = pl.ds(row(1) + half, half)
                F[h, second] = F[h, second] + RB[rd, h, g, 1]
                rs(rd, h, g, k0 + 5).start()
            if n in (2, 4):
                for k in (2, 3, 4, 5):
                    rs(rd, h, g, k0 + k).wait_recv()
                first, second = pl.ds(row(0), half), pl.ds(row(0) + half, half)
                F[h, first] = F[h, first] + RB[rd, h, g, 3] + RB[rd, h, g, 4]
                F[h, second] = F[h, second] + RB[rd, h, g, 2] + RB[rd, h, g, 5]
            if n in (0, 2):
                for k in range(4):
                    rs(rd, h, g, (0 if n == 0 else 6) + k).start()

    def rs_sent(rd):
        for h in (0, 1):
            for g in (0, 1):
                for k in range(12):
                    rs(rd, h, g, k).wait_send()

    def ar(n, k):
        src = AS if k < 3 else AS2
        o = k % 3 + 1
        dev = at_views(0, x + o, y) if k < 3 else at_views(0, x, y + o)
        return pltpu.make_async_remote_copy(
            src_ref=src.at[n], dst_ref=AR.at[n, k],
            send_sem=ar_s.at[n, k], recv_sem=ar_r.at[n, k],
            device_id=dev, device_id_type=pl.DeviceIdType.MESH,
        )

    def ar_start(n, value):
        AS[n] = value
        for k in range(3):
            ar(n, k).start()

    def ar_mid(n):
        for k in range(3):
            ar(n, k).wait_recv()
        AS2[n] = AS[n] + AR[n, 0] + AR[n, 1] + AR[n, 2]
        for k in range(3, 6):
            ar(n, k).start()

    def ar_end(n):
        for k in range(3, 6):
            ar(n, k).wait_recv()
        total = AS2[n] + AR[n, 3] + AR[n, 4] + AR[n, 5]
        for k in range(6):
            ar(n, k).wait_send()
        return lane_total(total)

    def en(n, o):
        to = lax.rem(e + o, 8)
        dst = T if n == 0 else MB
        return pltpu.make_async_remote_copy(
            src_ref=TP.at[n, to], dst_ref=dst.at[e],
            send_sem=en_s.at[n, o], recv_sem=en_r.at[n, o],
            device_id={"energy": to}, device_id_type=pl.DeviceIdType.MESH,
        )

    def own_rows(h, g):
        p, s = coord[g]
        return pl.ds(g * 128 + (s * 4 + p) * 8, 8)

    for h in (0, 1):
        for blk in range(16):
            piece = x0[:, blk * 256 + h * 128 : blk * 256 + h * 128 + 128]
            X[h, blk // 8, blk % 8] = piece
        for g in (0, 1):
            V[0][h][own_rows(h, g)] = X[h, g]
        ag_step(0, h, 0)

    for to in range(8):
        for i in (0, 1):
            for h in (0, 1):
                cols = slice(i * 256 + h * 128, i * 256 + h * 128 + 128)
                rows = slice(to * 8, to * 8 + 8)
                TP[0, to, i, h] = split[0, rows, cols] - dual[0, rows, cols]
    T[e] = TP[0, e]
    for o in range(1, 8):
        en(0, o).start()

    R[0] = jnp.zeros((8, 128), F32)

    def convert(c, carry):
        slot = lax.rem(c, NSTAGE)
        tile_copy(c, slot).wait()
        b = c // 6
        for u in range(CH // 2):
            jp = (c % 6) * (CH // 2) + u
            for h in (0, 1):
                for t in (0, 1):
                    hi, lo = split2(stage[slot, 2 * u + t, :, h * 128 : h * 128 + 128])
                    W[h, b, jp, 0:128, t * 128 : t * 128 + 128] = hi
                    W[h, b, jp, 128:256, t * 128 : t * 128 + 128] = lo

        @pl.when(c + NSTAGE < 24)
        def _():
            tile_copy(c + NSTAGE, slot).start()

        return carry

    def fwd(rd, h, lo_b, hi_b):
        def body(b, carry):
            acc = jnp.zeros((16, 256), F32)
            for jp in range(24):
                i = b * 48 + 2 * jp
                v0 = V[rd][h][idx[i]]
                v1 = V[rd][h][idx[i + 1]]
                hi, lo = split2(jnp.concatenate([v0, v1], axis=1))
                acc = acc + lax.dot_general(
                    jnp.concatenate([hi, lo], axis=0), W[h, b, jp],
                    (((1,), (1,)), ((), ())), preferred_element_type=F32,
                )
            both = acc[0:8] + acc[8:16]
            part = both[:, 0:128] + both[:, 128:256]
            if h == 0:
                Pq[b] = part
            else:
                Pq[b] = Pq[b] + part
            return carry

        lax.fori_loop(lo_b, hi_b, body, 0)

    def bwd(h, lo_b, hi_b):
        def body(b, carry):
            lhs = WL[b]
            for jp in range(24):
                i = b * 48 + 2 * jp
                out = lax.dot_general(
                    lhs, W[h, b, jp], (((1,), (0,)), ((), ())), preferred_element_type=F32
                )
                both = out[0:8] + out[8:16]
                R[i + 1] = both[:, 0:128] + R[idx[192 + i]]
                R[i + 2] = both[:, 128:256] + R[idx[193 + i]]
            return carry

        lax.fori_loop(lo_b, hi_b, body, 0)

    def scatter(h):
        def body(n, carry):
            for j in range(8):
                F[h, n * 8 + j] = R[idx[384 + n * 8 + j]]
            return carry

        lax.fori_loop(0, 32, body, 0)

    lane = lax.broadcasted_iota(jnp.int32, (8, 128), 1)

    def scale(b):
        return jnp.where(lane < counts[b], wts[:, b * 128 : b * 128 + 128], 0.0)

    def squares(v):
        return jnp.sum(v * v, axis=0)

    lax.fori_loop(0, 6, convert, 0)
    ag_step(0, 0, 1)
    ag_step(0, 1, 1)
    lax.fori_loop(6, 12, convert, 0)
    ag_step(0, 0, 2)
    ag_step(0, 1, 2)
    lax.fori_loop(12, 18, convert, 0)
    ag_step(0, 0, 3)
    lax.fori_loop(18, 24, convert, 0)
    ag_step(0, 1, 3)

    rr = None
    for rd in range(4):
        last = rd == 3
        if rd > 0:
            ag_step(rd, 0, 2)
            ag_step(rd, 1, 1)
            ag_step(rd, 0, 3)
            ag_step(rd, 1, 2)
        ag_step(rd, 0, 4)
        fwd(rd, 0, 0, 2)
        if rd > 0:
            ar_mid(2 * rd - 2)
            ag_step(rd, 1, 3)
        fwd(rd, 0, 2, 4)
        ag_step(rd, 1, 4)
        fwd(rd, 1, 0, 4)
        ag_sent(rd)
        if rd == 0:
            for b in range(4):
                w = scale(b) * (sino[:, b * 128 : b * 128 + 128] - Pq[b])
                hi, lo = split2(w)
                WL[b] = jnp.concatenate(
                    [jnp.concatenate([hi, hi], axis=1), jnp.concatenate([lo, lo], axis=1)], axis=0
                )
        else:
            rr_new = ar_end(2 * rd - 2)
            curv = jnp.zeros((8, 128), F32)
            if rd > 1:
                beta = rr_new / rr
            rr = rr_new
            for h in (0, 1):
                for g in (0, 1):
                    r_own = V[rd][h][own_rows(h, g)]
                    d_own = r_own if rd == 1 else r_own + beta * D[h, g]
                    D[h, g] = d_own
                    curv = curv + PENALTY * squares(d_own)
            for b in range(4):
                q = Pq[b] if rd == 1 else Pq[b] + beta * Q[b]
                Q[b] = q
                w = scale(b) * q
                curv = curv + w * q
                if not last:
                    hi, lo = split2(w)
                    WL[b] = jnp.concatenate(
                        [jnp.concatenate([hi, hi], axis=1), jnp.concatenate([lo, lo], axis=1)], axis=0
                    )
            ar_start(2 * rd - 1, curv)
        if not last:
            bwd(0, 0, 4)
            scatter(0)
            rs_step(rd, 0, 0)
            if rd > 0:
                ar_mid(2 * rd - 1)
            bwd(1, 0, 2)
            rs_step(rd, 0, 1)
            bwd(1, 2, 4)
            scatter(1)
            rs_step(rd, 1, 0)
            rs_step(rd, 0, 2)
            rs_step(rd, 1, 1)
            if rd > 0:
                alpha = rr / ar_end(2 * rd - 1)
            else:
                for o in range(1, 8):
                    en(0, o).wait_recv()
            rs_step(rd, 0, 3)
            rs_step(rd, 1, 2)
            norm = jnp.zeros((8, 128), F32)
            for h in (0, 1):
                rs_step(rd, h, 4)
                for g in (0, 1):
                    summed = F[h, own_rows(h, g)]
                    if rd == 0:
                        anchor = T[g * 4 : g * 4 + 4, :, h].reshape(8, 8, 128)
                        r_own = summed + PENALTY * (anchor - X[h, g])
                    else:
                        d_own = D[h, g]
                        r_own = V[rd][h][own_rows(h, g)] - alpha * (summed + PENALTY * d_own)
                        X[h, g] = X[h, g] + alpha * d_own
                    V[rd + 1][h][own_rows(h, g)] = r_own
                    norm = norm + squares(r_own)
                ag_step(rd + 1, h, 0)
                if h == 0:
                    rs_step(rd, 1, 3)
                    ag_step(rd + 1, 0, 1)
            ar_start(2 * rd, norm)
            rs_sent(rd)
        else:
            ar_mid(2 * rd - 1)
            alpha = rr / ar_end(2 * rd - 1)
            for h in (0, 1):
                for g in (0, 1):
                    X[h, g] = X[h, g] + alpha * D[h, g]
    for to in range(8):
        for i in (0, 1):
            for h in (0, 1):
                blk = 2 * to + i
                TP[1, to, i, h] = X[h, blk // 8, blk % 8]
    for o in range(1, 8):
        en(1, o).start()
    MB[e] = TP[1, e]
    for h in (0, 1):
        for blk in range(16):
            vol_out[:, blk * 256 + h * 128 : blk * 256 + h * 128 + 128] = X[h, blk // 8, blk % 8]
    for o in range(1, 8):
        en(1, o).wait_recv()
    mb_out[...] = MB[...]
    for n in (0, 1):
        for o in range(1, 8):
            en(n, o).wait_send()


def shrink_kernel(mb, dual, split_out, dual_out, M, B):
    lane = lax.broadcasted_iota(jnp.int32, (64, 128), 1)
    row = lax.broadcasted_iota(jnp.int32, (64, 128), 0)
    left = lane < 64
    for i in (0, 1):
        for h in (0, 1):
            n = i * 2 + h
            b = mb[:, i, h].reshape(64, 128) + dual[0, :, n * 128 : n * 128 + 128]
            B[n] = b
            turned = pltpu.roll(b, 64, axis=1)
            for side in (0, 1):
                one = jnp.where(left if side == 0 else lane >= 64, b, 0.0)
                gram = lax.dot_general(
                    one, jnp.concatenate([one, one], axis=0), (((1,), (1,)), ((), ())),
                    precision=lax.Precision.HIGHEST, preferred_element_type=F32,
                )
                gram = gram + jnp.where(lane == row, SHRINK, 0.0)
                M[n * 2 + side] = jnp.where(left, gram, turned if side == 0 else b)

    def step(k, carry):
        pick = jnp.full((64, 128), k, jnp.int32)
        for p in range(8):
            m = M[p]
            line = M[p, pl.ds(k, 1), :]
            col = jnp.take_along_axis(m, pick, axis=1)
            pivot = jnp.take_along_axis(jnp.broadcast_to(line, (8, 128)), pick[0:8], axis=1)[0:1]
            scaled = line / pivot
            M[p] = jnp.where(row == k, jnp.broadcast_to(scaled, (64, 128)), m - col * scaled)
        return carry

    lax.fori_loop(0, 64, step, 0)
    for i in (0, 1):
        for h in (0, 1):
            n = i * 2 + h
            solved = jnp.where(left, pltpu.roll(M[n * 2], 64, axis=1), M[n * 2 + 1])
            b = B[n]
            cols = slice(n * 128, n * 128 + 128)
            new_split = b - SHRINK * solved
            split_out[0, :, cols] = new_split
            dual_out[0, :, cols] = b - new_split


def local(tiles, tile_blocks, counts, sino, wts, x0, split, dual):
    n = tile_blocks.reshape(-1)
    tiles_here = n.shape[0]
    src, blk = n // 16, n % 16
    g = blk // 8
    place = jnp.where(g == 0, src, (src % 4) * 4 + src // 4)
    vrow = g * 128 + place * 8 + blk % 8
    order = jnp.arange(tiles_here, dtype=jnp.int32)
    same = (n[:, None] == n[None, :]) & (order[None, :] < order[:, None])
    prev = jnp.max(jnp.where(same, order[None, :] + 1, 0), axis=1)
    rows = jnp.arange(256, dtype=jnp.int32)
    final = jnp.max(jnp.where(rows[:, None] == vrow[None, :], order[None, :] + 1, 0), axis=1)
    idx = jnp.concatenate([vrow, prev, final])
    vmem = pl.BlockSpec(memory_space=pltpu.VMEM)
    smem = pl.BlockSpec(memory_space=pltpu.SMEM)
    volume, mb = pl.pallas_call(
        main_kernel,
        out_shape=(
            jax.ShapeDtypeStruct((8, 4096), F32),
            jax.ShapeDtypeStruct((8, 2, 2, 8, 128), F32),
        ),
        in_specs=[smem, smem, pl.BlockSpec(memory_space=pl.ANY)] + [vmem] * 5,
        out_specs=(vmem, vmem),
        scratch_shapes=[
            pltpu.VMEM((2, 4, 24, 256, 256), BF16),
            pltpu.VMEM((NSTAGE, CH, 128, 256), F32),
            *[pltpu.VMEM((256, 8, 128), F32)] * 8,
            pltpu.VMEM((2, 256, 8, 128), F32),
            pltpu.VMEM((3, 2, 2, 6, 16, 8, 128), F32),
            pltpu.VMEM((3, 2, 2, 6, 4, 8, 128), F32),
            pltpu.VMEM((193, 8, 128), F32),
            pltpu.VMEM((2, 2, 8, 8, 128), F32),
            pltpu.VMEM((2, 2, 8, 8, 128), F32),
            pltpu.VMEM((8, 2, 2, 8, 128), F32),
            pltpu.VMEM((2, 8, 2, 2, 8, 128), F32),
            pltpu.VMEM((8, 2, 2, 8, 128), F32),
            pltpu.VMEM((4, 8, 128), F32),
            pltpu.VMEM((4, 8, 128), F32),
            pltpu.VMEM((4, 16, 256), BF16),
            pltpu.VMEM((6, 8, 128), F32),
            pltpu.VMEM((6, 8, 128), F32),
            pltpu.VMEM((6, 6, 8, 128), F32),
            pltpu.SemaphoreType.DMA((NSTAGE,)),
            pltpu.SemaphoreType.DMA((4, 2, 2, 8)),
            pltpu.SemaphoreType.DMA((4, 2, 2, 8)),
            pltpu.SemaphoreType.DMA((3, 2, 2, 12)),
            pltpu.SemaphoreType.DMA((3, 2, 2, 12)),
            pltpu.SemaphoreType.DMA((6, 6)),
            pltpu.SemaphoreType.DMA((6, 6)),
            pltpu.SemaphoreType.DMA((2, 8)),
            pltpu.SemaphoreType.DMA((2, 8)),
        ],
        compiler_params=pltpu.CompilerParams(
            collective_id=0, has_side_effects=True, vmem_limit_bytes=56 * 1024 * 1024
        ),
        name="solve",
    )(idx, counts, tiles, sino, wts, x0, split, dual)
    new_split, new_dual = pl.pallas_call(
        shrink_kernel,
        out_shape=(jax.ShapeDtypeStruct((1, 64, 512), F32),) * 2,
        in_specs=[vmem, vmem],
        out_specs=(vmem, vmem),
        scratch_shapes=[pltpu.VMEM((8, 64, 128), F32), pltpu.VMEM((4, 64, 128), F32)],
        compiler_params=pltpu.CompilerParams(vmem_limit_bytes=16 * 1024 * 1024),
        name="shrink",
    )(mb, dual)
    return volume, new_split, new_dual


def solution(mesh):
    placed = (
        P("views", None, None, None),
        P("views", None),
        P("views"),
        P("energy", "views"),
        P("energy", "views"),
        P("energy", "views"),
        P("views", None, "energy"),
        P("views", None, "energy"),
    )
    return jax.shard_map(
        local,
        mesh=mesh,
        in_specs=placed,
        out_specs=(P("energy", "views"), P("views", None, "energy"), P("views", None, "energy")),
        check_vma=False,
    )
```

time: 1060 us -> 232 us (0.22); the launches traced: 1050 us -> 232 us
  waiting for transfers between devices: 494 us -> 0 us
  Pallas kernels: 0 us -> 227 us
  other arithmetic: 181 us -> 1.02 us
  blocking collectives: 161 us -> 0 us
  matrix products: 154 us -> 0 us
  local copies, waits for them, and re-layouts: 27 us -> 3.27 us
  starting transfers between devices: 15.6 us -> 0 us
  between operations: 14.8 us -> 0.67 us
    reduce_scatter x4 -> x0, waiting for transfers between devices: 280 us -> none  [normal_map(): lax.psum_scatter(partial_sum, 'views', scatter_dimension=1, tiled=True)]
    pallas_call x0 -> x2, Pallas kernels: none -> 227 us  [the longest x1 182 us: local(): pl.pallas_call(main_kernel, out_shape=(jax.ShapeDtypeStruct((8, 4096), F3...]
    all_gather x4 -> x0, waiting for transfers between devices: 208 us -> none  [normal_map(): gathered = lax.all_gather(vector, 'views', axis=1, tiled=True)]
    dot_general x9 -> x0, matrix products: 153 us -> none  [the longest x4 92.2 us: forward(): jnp.einsum('crtv,rtkv->crk', columns, projector_tiles, precision=exact_mode)]
    psum x5 -> x0, blocking collectives: 150 us -> none  [the longest x3 87.9 us: norm_total(): return lax.psum(jnp.sum(jnp.square(vector), axis=1), 'views')]
    another operation x7 -> x0, other arithmetic: 86.5 us -> none  [the longest x4 47.1 us: shrink_patches(): factor = jnp.linalg.cholesky(shifted)]
    scatter-add x4 -> x0, other arithmetic: 61.9 us -> none  [backward(): block_grid.at[:, tile_blocks.reshape(-1)]]
    unnamed x1 -> x0, other arithmetic: 19.4 us -> none
  transfers between devices with their start and end apart: 9 -> 0, of which waited for: 9 -> 0; matrix products, arithmetic and copies ran while one was open for 0% -> 0% of each run, Pallas kernels for 0% -> 0%
where the time goes in v1:
time: 232 us
  Pallas kernels  227 us (98%)
  local copies, waits for them, and re-layouts  3.27 us (1%)
    pallas_call x1, Pallas kernels, local(): pl.pallas_call(main_kernel, out_shape=(jax.ShapeDtypeStruct((8, 4096), F3...  182 us
    pallas_call x1, Pallas kernels, local(): pl.pallas_call(shrink_kernel, out_shape=(jax.ShapeDtypeStruct((1, 64, 512...  44.8 us

profile of v1, /device:TPU:1, one launch (start us, length us, event | category | flops | bytes accessed | tf_op | source)
XLA Modules:
  0.0 231.6 jit_solution(14625896161811255899)
XLA Ops:
  0.6 0.0 copy-start
  0.6 0.8 reshape.124
  1.5 0.2 select_reduce_fusion.1
  1.7 0.1 select_reduce_fusion
  1.8 0.7 pad_add_fusion.idx
  2.5 181.9 %solve.1 = (f32[8,4096]{1,0:T(8,128)}, f32[8,2,2,8,128]{4,3,2,1,0:T(8,128)}) custom-call(s32[640]{0:T(1024)} %pad_add_fusion.idx, s32[4]{0:T(128)} %counts.1, f32[4,48,128,256]{3,2,1,0:T(8,128)} %tiles.1, f32[8,512]{1,0:T(8,128)} %sino.1, f32[8,512]{1,0:T(8,128)} %wts.1, f32[8,4096]{1,0:T(8,128)} %x0.1, f32[1,64,512]{2,1,0:T(8,128)} %split.1, f32[1,64,512]{2,1,0:T(8,128)} %dual.3), custom_call_target="tpu_custom_call" | custom-call | tf_op jit(solution)/shard_map/solve/pallas_call | solution.py:497
  184.3 0.0 copy-done
  184.3 0.0 copy-start.1
  184.3 0.9 copy-done.1
  185.2 44.8 %shrink.1 = (f32[1,64,512]{2,1,0:T(8,128)}, f32[1,64,512]{2,1,0:T(8,128)}) custom-call(f32[8,2,2,8,128]{4,3,2,1,0:T(8,128)S(1)} %copy-done.1, f32[1,64,512]{2,1,0:T(8,128)S(1)} %copy-done), custom_call_target="tpu_custom_call" | custom-call | tf_op jit(solution)/shard_map/shrink/pallas_call | solution.py:539
  230.0 1.6 copy.12
  (1 shorter events, 0.0 us)
Async XLA Ops:
  0.6 183.7 %copy-start = (f32[1,64,512]{2,1,0:T(8,128)S(1)}, f32[1,64,512]{2,1,0:T(8,128)}, u32[]{:S(2)}) copy-start(f32[1,64,512]{2,1,0:T(8,128)} %dual.3) | copy-start | bytes 393220
  184.3 0.9 copy-start.1

commit v2 on v1

--- a/solution.py
+++ b/solution.py
@@ -62,122 +62,83 @@
 
     def ag(rd, h, g, k):
         p, s = coord[g]
-        base = g * 128
-        own = base + (s * 4 + p) * 8
-
-        def chunk(pp):
-            return base + (s * 4 + lax.rem(pp + 4, 4)) * 8
-
-        def line(ss):
-            return base + lax.rem(ss + 4, 4) * 32
-
-        src, size, dev = {
-            0: (own, 8, (p + 1, s)),
-            1: (own, 8, (p - 1, s)),
-            2: (chunk(p - 1), 4, (p + 1, s)),
-            3: (chunk(p + 1) + 4, 4, (p - 1, s)),
-            4: (line(s), 32, (p, s + 1)),
-            5: (line(s), 32, (p, s - 1)),
-            6: (line(s - 1), 16, (p, s + 1)),
-            7: (line(s + 1) + 16, 16, (p, s - 1)),
-        }[k]
-        ref = V[rd][h].at[pl.ds(src, size)]
+        base, o = g * 128, k % 3 + 1
+        src, size, dst, dev = (
+            (0, 8, (4 - o) * 8, (p + o, s)),
+            (0, 8, (4 - o) * 32, (p, s + o)),
+            (8, 24, (4 - o) * 32 + 8, (p, s + o)),
+        )[k // 3]
         return pltpu.make_async_remote_copy(
-            src_ref=ref, dst_ref=ref,
+            src_ref=V[rd][h].at[pl.ds(base + src, size)], dst_ref=V[rd][h].at[pl.ds(base + dst, size)],
             send_sem=ag_s.at[rd, h, g, k], recv_sem=ag_r.at[rd, h, g, k],
             device_id=at_views(g, *dev), device_id_type=pl.DeviceIdType.MESH,
         )
 
     def ag_step(rd, h, n):
-        for g in (0, 1):
-            if n > 0:
-                ag(rd, h, g, 2 * n - 2).wait_recv()
-                ag(rd, h, g, 2 * n - 1).wait_recv()
-            if n < 4:
-                ag(rd, h, g, 2 * n).start()
-                ag(rd, h, g, 2 * n + 1).start()
+        if n == 0:
+            for k in (1, 0, 2, 4, 3, 5):
+                for g in (0, 1):
+                    ag(rd, h, g, k).start()
+        if n == 1:
+            for g in (0, 1):
+                for k in (0, 1, 2):
+                    ag(rd, h, g, k).wait_recv()
+                for k in (7, 6, 8):
+                    ag(rd, h, g, k).start()
+        if n == 2:
+            for g in (0, 1):
+                for k in range(3, 9):
+                    ag(rd, h, g, k).wait_recv()
 
     def ag_sent(rd):
         for h in (0, 1):
             for g in (0, 1):
-                for k in range(8):
+                for k in range(9):
                     ag(rd, h, g, k).wait_send()
 
     def rs(rd, h, g, k):
         p, s = coord[g]
-        base = g * 128
-        kk = k % 6
-        if k < 6:
-            half = 16
-
-            def row(o):
-                return base + lax.rem(s + o + 4, 4) * 32
-
-            def dev(o):
-                return at_views(g, p, s + o)
-
-            land = RB1.at[rd, h, g, kk]
-        else:
-            half = 4
-
-            def row(o):
-                return base + (s * 4 + lax.rem(p + o + 4, 4)) * 8
-
-            def dev(o):
-                return at_views(g, p + o, s)
-
-            land = RB2.at[rd, h, g, kk]
-        src, to = (
-            (row(2), -1),
-            (row(2) + half, 1),
-            (row(-1) + half, -1),
-            (row(1), 1),
-            (row(-1), -1),
-            (row(1) + half, 1),
-        )[kk]
+        base, o = g * 128, k % 3 + 1
+        src, size, dev = (
+            (o * 32 + 8, 24, (p, s + o)),
+            (o * 32, 8, (p, s + o)),
+            (o * 8, 8, (p + o, s)),
+        )[k // 3]
+        land = RB1.at[rd, h, g, k] if k < 3 else RB2.at[rd, h, g, k - 3]
         return pltpu.make_async_remote_copy(
-            src_ref=F.at[h, pl.ds(src, half)], dst_ref=land,
+            src_ref=F.at[h, pl.ds(base + src, size)], dst_ref=land,
             send_sem=rs_s.at[rd, h, g, k], recv_sem=rs_r.at[rd, h, g, k],
-            device_id=dev(to), device_id_type=pl.DeviceIdType.MESH,
+            device_id=at_views(g, *dev), device_id_type=pl.DeviceIdType.MESH,
         )
 
     def rs_step(rd, h, n):
-        for g in (0, 1):
-            p, s = coord[g]
-            base = g * 128
-            if n < 2 or n == 2:
-                half, RB, k0 = 16, RB1, 0
-
-                def row(o):
-                    return base + lax.rem(s + o + 4, 4) * 32
-            else:
-                half, RB, k0 = 4, RB2, 6
-
-                def row(o):
-                    return base + (s * 4 + lax.rem(p + o + 4, 4)) * 8
-            if n in (1, 3):
-                rs(rd, h, g, k0).wait_recv()
-                first = pl.ds(row(-1), half)
-                F[h, first] = F[h, first] + RB[rd, h, g, 0]
-                rs(rd, h, g, k0 + 4).start()
-                rs(rd, h, g, k0 + 1).wait_recv()
-                second = pl.ds(row(1) + half, half)
-                F[h, second] = F[h, second] + RB[rd, h, g, 1]
-                rs(rd, h, g, k0 + 5).start()
-            if n in (2, 4):
-                for k in (2, 3, 4, 5):
-                    rs(rd, h, g, k0 + k).wait_recv()
-                first, second = pl.ds(row(0), half), pl.ds(row(0) + half, half)
-                F[h, first] = F[h, first] + RB[rd, h, g, 3] + RB[rd, h, g, 4]
-                F[h, second] = F[h, second] + RB[rd, h, g, 2] + RB[rd, h, g, 5]
-            if n in (0, 2):
-                for k in range(4):
-                    rs(rd, h, g, (0 if n == 0 else 6) + k).start()
+        if n == 0:
+            for k in (1, 0, 2, 4, 3, 5):
+                for g in (0, 1):
+                    rs(rd, h, g, k).start()
+        if n == 1:
+            for g in (0, 1):
+                for k in (0, 1, 2):
+                    rs(rd, h, g, k).wait_recv()
+                line = pl.ds(g * 128 + 8, 24)
+                F[h, line] = F[h, line] + RB1[rd, h, g, 0] + RB1[rd, h, g, 1] + RB1[rd, h, g, 2]
+                for k in (7, 6, 8):
+                    rs(rd, h, g, k).start()
+        if n == 2:
+            for g in (0, 1):
+                for k in range(3, 9):
+                    rs(rd, h, g, k).wait_recv()
+
+    def rs_total(rd, h, g):
+        total = F[h, own_rows(g)]
+        for k in range(6):
+            total = total + RB2[rd, h, g, k]
+        return total
 
     def rs_sent(rd):
         for h in (0, 1):
             for g in (0, 1):
-                for k in range(12):
+                for k in range(9):
                     rs(rd, h, g, k).wait_send()
 
     def ar(n, k):
@@ -219,16 +180,15 @@
             device_id={"energy": to}, device_id_type=pl.DeviceIdType.MESH,
         )
 
-    def own_rows(h, g):
-        p, s = coord[g]
-        return pl.ds(g * 128 + (s * 4 + p) * 8, 8)
+    def own_rows(g):
+        return pl.ds(g * 128, 8)
 
     for h in (0, 1):
         for blk in range(16):
             piece = x0[:, blk * 256 + h * 128 : blk * 256 + h * 128 + 128]
             X[h, blk // 8, blk % 8] = piece
         for g in (0, 1):
-            V[0][h][own_rows(h, g)] = X[h, g]
+            V[0][h][own_rows(g)] = X[h, g]
         ag_step(0, h, 0)
 
     for to in range(8):
@@ -314,32 +274,20 @@
     def squares(v):
         return jnp.sum(v * v, axis=0)
 
-    lax.fori_loop(0, 6, convert, 0)
+    lax.fori_loop(0, 10, convert, 0)
     ag_step(0, 0, 1)
     ag_step(0, 1, 1)
-    lax.fori_loop(6, 12, convert, 0)
-    ag_step(0, 0, 2)
-    ag_step(0, 1, 2)
-    lax.fori_loop(12, 18, convert, 0)
-    ag_step(0, 0, 3)
-    lax.fori_loop(18, 24, convert, 0)
-    ag_step(0, 1, 3)
+    lax.fori_loop(10, 24, convert, 0)
 
     rr = None
     for rd in range(4):
         last = rd == 3
-        if rd > 0:
-            ag_step(rd, 0, 2)
-            ag_step(rd, 1, 1)
-            ag_step(rd, 0, 3)
-            ag_step(rd, 1, 2)
-        ag_step(rd, 0, 4)
+        ag_step(rd, 0, 2)
         fwd(rd, 0, 0, 2)
         if rd > 0:
             ar_mid(2 * rd - 2)
-            ag_step(rd, 1, 3)
         fwd(rd, 0, 2, 4)
-        ag_step(rd, 1, 4)
+        ag_step(rd, 1, 2)
         fwd(rd, 1, 0, 4)
         ag_sent(rd)
         if rd == 0:
@@ -357,7 +305,7 @@
             rr = rr_new
             for h in (0, 1):
                 for g in (0, 1):
-                    r_own = V[rd][h][own_rows(h, g)]
+                    r_own = V[rd][h][own_rows(g)]
                     d_own = r_own if rd == 1 else r_own + beta * D[h, g]
                     D[h, g] = d_own
                     curv = curv + PENALTY * squares(d_own)
@@ -376,41 +324,37 @@
             bwd(0, 0, 4)
             scatter(0)
             rs_step(rd, 0, 0)
+            bwd(1, 0, 2)
             if rd > 0:
                 ar_mid(2 * rd - 1)
-            bwd(1, 0, 2)
-            rs_step(rd, 0, 1)
             bwd(1, 2, 4)
             scatter(1)
             rs_step(rd, 1, 0)
-            rs_step(rd, 0, 2)
+            rs_step(rd, 0, 1)
             rs_step(rd, 1, 1)
             if rd > 0:
                 alpha = rr / ar_end(2 * rd - 1)
             else:
                 for o in range(1, 8):
                     en(0, o).wait_recv()
-            rs_step(rd, 0, 3)
-            rs_step(rd, 1, 2)
             norm = jnp.zeros((8, 128), F32)
             for h in (0, 1):
-                rs_step(rd, h, 4)
+                rs_step(rd, h, 2)
                 for g in (0, 1):
-                    summed = F[h, own_rows(h, g)]
+                    summed = rs_total(rd, h, g)
                     if rd == 0:
                         anchor = T[g * 4 : g * 4 + 4, :, h].reshape(8, 8, 128)
                         r_own = summed + PENALTY * (anchor - X[h, g])
                     else:
                         d_own = D[h, g]
-                        r_own = V[rd][h][own_rows(h, g)] - alpha * (summed + PENALTY * d_own)
+                        r_own = V[rd][h][own_rows(g)] - alpha * (summed + PENALTY * d_own)
                         X[h, g] = X[h, g] + alpha * d_own
-                    V[rd + 1][h][own_rows(h, g)] = r_own
+                    V[rd + 1][h][own_rows(g)] = r_own
                     norm = norm + squares(r_own)
                 ag_step(rd + 1, h, 0)
-                if h == 0:
-                    rs_step(rd, 1, 3)
-                    ag_step(rd + 1, 0, 1)
             ar_start(2 * rd, norm)
+            ag_step(rd + 1, 0, 1)
+            ag_step(rd + 1, 1, 1)
             rs_sent(rd)
         else:
             ar_mid(2 * rd - 1)
@@ -437,7 +381,14 @@
             en(n, o).wait_send()
 
 
-def shrink_kernel(mb, dual, split_out, dual_out, M, B):
+def split3(v):
+    a = v.astype(BF16)
+    rest = v - a.astype(F32)
+    b = rest.astype(BF16)
+    return a, b, (rest - b.astype(F32)).astype(BF16)
+
+
+def shrink_kernel(mb, dual, split_out, dual_out, M, B, GA, GB):
     lane = lax.broadcasted_iota(jnp.int32, (64, 128), 1)
     row = lax.broadcasted_iota(jnp.int32, (64, 128), 0)
     left = lane < 64
@@ -456,18 +407,42 @@
                 gram = gram + jnp.where(lane == row, SHRINK, 0.0)
                 M[n * 2 + side] = jnp.where(left, gram, turned if side == 0 else b)
 
-    def step(k, carry):
-        pick = jnp.full((64, 128), k, jnp.int32)
+    place = lax.broadcasted_iota(jnp.int32, (8, 128), 0)
+    none = jnp.zeros((8, 128), F32)
+    blank = jnp.zeros((16, 128), BF16)
+    GA[...] = jnp.zeros_like(GA)
+    GB[...] = jnp.zeros_like(GB)
+    for kb in range(8):
+        heads = [M[p, kb * 8 : kb * 8 + 8, :] for p in range(8)]
+        for j in range(8):
+            for p in range(8):
+                m = heads[p]
+                k = kb * 8 + j
+                col = jnp.broadcast_to(m[:, k : k + 1], (8, 128))
+                scaled = m[j : j + 1] / col[j : j + 1]
+                heads[p] = jnp.where(place == j, scaled, m - col * scaled)
+        top = slice(kb // 2 * 16, kb // 2 * 16 + 16)
+        low = slice(128 + kb // 2 * 16, 144 + kb // 2 * 16)
+        for p in range(8):
+            if kb % 2 == 0 and kb > 0:
+                for lines in (slice(kb // 2 * 16 - 16, kb // 2 * 16), slice(112 + kb // 2 * 16, 128 + kb // 2 * 16)):
+                    GA[p, lines, 0:128] = blank
+                    GA[p, lines, 128:256] = blank
+                    GB[p, lines, :] = blank
+            pair = [heads[p], none] if kb % 2 == 0 else [none, heads[p]]
+            h1, h2, h3 = split3(jnp.concatenate(pair, axis=0))
+            for lines in (top, low):
+                GA[p, lines, 0:128] = h1
+                GA[p, lines, 128:256] = h2
+            GB[p, top, :] = h3
+            GB[p, low, :] = h1
         for p in range(8):
             m = M[p]
-            line = M[p, pl.ds(k, 1), :]
-            col = jnp.take_along_axis(m, pick, axis=1)
-            pivot = jnp.take_along_axis(jnp.broadcast_to(line, (8, 128)), pick[0:8], axis=1)[0:1]
-            scaled = line / pivot
-            M[p] = jnp.where(row == k, jnp.broadcast_to(scaled, (64, 128)), m - col * scaled)
-        return carry
-
-    lax.fori_loop(0, 64, step, 0)
+            m1, m2, m3 = split3(m)
+            big = jnp.dot(jnp.concatenate([m1, m2], axis=1), GA[p], preferred_element_type=F32)
+            small = jnp.dot(jnp.concatenate([m1, m3], axis=1), GB[p], preferred_element_type=F32)
+            M[p] = m - (big[:, 0:128] + (big[:, 128:256] + small))
+            M[p, kb * 8 : kb * 8 + 8, :] = heads[p]
     for i in (0, 1):
         for h in (0, 1):
             n = i * 2 + h
@@ -484,7 +459,9 @@
     tiles_here = n.shape[0]
     src, blk = n // 16, n % 16
     g = blk // 8
-    place = jnp.where(g == 0, src, (src % 4) * 4 + src // 4)
+    me = lax.axis_index("views")
+    across, down = (src - me) % 4, (src // 4 - me // 4) % 4
+    place = jnp.where(g == 0, down * 4 + across, across * 4 + down)
     vrow = g * 128 + place * 8 + blk % 8
     order = jnp.arange(tiles_here, dtype=jnp.int32)
     same = (n[:, None] == n[None, :]) & (order[None, :] < order[:, None])
@@ -507,8 +484,8 @@
             pltpu.VMEM((NSTAGE, CH, 128, 256), F32),
             *[pltpu.VMEM((256, 8, 128), F32)] * 8,
             pltpu.VMEM((2, 256, 8, 128), F32),
-            pltpu.VMEM((3, 2, 2, 6, 16, 8, 128), F32),
-            pltpu.VMEM((3, 2, 2, 6, 4, 8, 128), F32),
+            pltpu.VMEM((3, 2, 2, 3, 24, 8, 128), F32),
+            pltpu.VMEM((3, 2, 2, 6, 8, 8, 128), F32),
             pltpu.VMEM((193, 8, 128), F32),
             pltpu.VMEM((2, 2, 8, 8, 128), F32),
             pltpu.VMEM((2, 2, 8, 8, 128), F32),
@@ -522,10 +499,10 @@
             pltpu.VMEM((6, 8, 128), F32),
             pltpu.VMEM((6, 6, 8, 128), F32),
             pltpu.SemaphoreType.DMA((NSTAGE,)),
-            pltpu.SemaphoreType.DMA((4, 2, 2, 8)),
-            pltpu.SemaphoreType.DMA((4, 2, 2, 8)),
-            pltpu.SemaphoreType.DMA((3, 2, 2, 12)),
-            pltpu.SemaphoreType.DMA((3, 2, 2, 12)),
+            pltpu.SemaphoreType.DMA((4, 2, 2, 9)),
+            pltpu.SemaphoreType.DMA((4, 2, 2, 9)),
+            pltpu.SemaphoreType.DMA((3, 2, 2, 9)),
+            pltpu.SemaphoreType.DMA((3, 2, 2, 9)),
             pltpu.SemaphoreType.DMA((6, 6)),
             pltpu.SemaphoreType.DMA((6, 6)),
             pltpu.SemaphoreType.DMA((2, 8)),
@@ -541,7 +518,10 @@
         out_shape=(jax.ShapeDtypeStruct((1, 64, 512), F32),) * 2,
         in_specs=[vmem, vmem],
         out_specs=(vmem, vmem),
-        scratch_shapes=[pltpu.VMEM((8, 64, 128), F32), pltpu.VMEM((4, 64, 128), F32)],
+        scratch_shapes=[
+            pltpu.VMEM((8, 64, 128), F32), pltpu.VMEM((4, 64, 128), F32),
+            pltpu.VMEM((8, 256, 256), BF16), pltpu.VMEM((8, 256, 128), BF16),
+        ],
         compiler_params=pltpu.CompilerParams(vmem_limit_bytes=16 * 1024 * 1024),
         name="shrink",
     )(mb, dual)

time: 232 us -> 172 us (0.74)
  Pallas kernels: 227 us -> 166 us
    pallas_call x1, Pallas kernels: 44.8 us -> 8.75 us  [local(): pl.pallas_call(shrink_kernel, out_shape=(jax.ShapeDtypeStruct((1, 64, 512...]
    pallas_call x1, Pallas kernels: 182 us -> 158 us  [local(): pl.pallas_call(main_kernel, out_shape=(jax.ShapeDtypeStruct((8, 4096), F3...]
where the time goes in v2:
time: 172 us; the launch traced here: 171 us
  Pallas kernels  166 us (97%)
  local copies, waits for them, and re-layouts  3.27 us (2%)
    pallas_call x1, Pallas kernels, local(): pl.pallas_call(main_kernel, out_shape=(jax.ShapeDtypeStruct((8, 4096), F3...  158 us
    pallas_call x1, Pallas kernels, local(): pl.pallas_call(shrink_kernel, out_shape=(jax.ShapeDtypeStruct((1, 64, 512...  8.75 us

profile of v2, /device:TPU:1, one launch (start us, length us, event | category | flops | bytes accessed | tf_op | source)
XLA Modules:
  0.0 171.3 jit_solution(7408905743488906004)
XLA Ops:
  0.6 0.0 copy-start
  0.7 0.8 reshape.139
  1.5 0.2 select_reduce_fusion.1
  1.7 0.1 select_reduce_fusion
  1.8 0.7 pad_add_fusion.idx
  2.5 157.6 %solve.1 = (f32[8,4096]{1,0:T(8,128)}, f32[8,2,2,8,128]{4,3,2,1,0:T(8,128)}) custom-call(s32[640]{0:T(1024)} %pad_add_fusion.idx, s32[4]{0:T(128)} %counts.1, f32[4,48,128,256]{3,2,1,0:T(8,128)} %tiles.1, f32[8,512]{1,0:T(8,128)} %sino.1, f32[8,512]{1,0:T(8,128)} %wts.1, f32[8,4096]{1,0:T(8,128)} %x0.1, f32[1,64,512]{2,1,0:T(8,128)} %split.1, f32[1,64,512]{2,1,0:T(8,128)} %dual.3), custom_call_target="tpu_custom_call" | custom-call | tf_op jit(solution)/shard_map/solve/pallas_call | solution.py:474
  160.1 0.0 copy-done
  160.1 0.0 copy-start.1
  160.1 0.9 copy-done.1
  161.0 8.8 %shrink.1 = (f32[1,64,512]{2,1,0:T(8,128)}, f32[1,64,512]{2,1,0:T(8,128)}) custom-call(f32[8,2,2,8,128]{4,3,2,1,0:T(8,128)S(1)} %copy-done.1, f32[1,64,512]{2,1,0:T(8,128)S(1)} %copy-done), custom_call_target="tpu_custom_call" | custom-call | tf_op jit(solution)/shard_map/shrink/pallas_call | solution.py:516
  169.7 1.6 copy.12
  (1 shorter events, 0.0 us)
Async XLA Ops:
  0.6 159.5 %copy-start = (f32[1,64,512]{2,1,0:T(8,128)S(1)}, f32[1,64,512]{2,1,0:T(8,128)}, u32[]{:S(2)}) copy-start(f32[1,64,512]{2,1,0:T(8,128)} %dual.3) | copy-start | bytes 393220
  160.1 0.9 copy-start.1

commit v3 on v2

--- a/solution.py
+++ b/solution.py
@@ -27,11 +27,11 @@
 
 def main_kernel(
     idx, counts, tiles, sino, wts, x0, split, dual,
-    vol_out, mb_out,
+    vol_out, mx_out, md_out, step_out,
     W, stage,
     V00, V01, V10, V11, V20, V21, V30, V31,
-    F, RB1, RB2, R, X, D, T, TP, MB, Pq, Q, WL, AS, AS2, AR,
-    dsem, ag_s, ag_r, rs_s, rs_r, ar_s, ar_r, en_s, en_r,
+    F, RB1, RB2, R, X, D, T, TP, MX, MD, MS, SD, Pq, Q, WL, AS, AS2, AR,
+    dsem, isem, ag_s, ag_r, rs_s, rs_r, ar_s, ar_r, en_s, en_r,
 ):
     V = ((V00, V01), (V10, V11), (V20, V21), (V30, V31))
     e = lax.axis_index("energy")
@@ -50,15 +50,18 @@
         pl.semaphore_signal(barrier, inc=1, device_id=at_views(0, x, y + o), device_id_type=pl.DeviceIdType.MESH)
     for o in range(1, 8):
         pl.semaphore_signal(barrier, inc=1, device_id={"energy": lax.rem(e + o, 8)}, device_id_type=pl.DeviceIdType.MESH)
-    pl.semaphore_wait(barrier, 13)
-
     def tile_copy(c, slot):
         return pltpu.make_async_copy(
             tiles.at[c // 6, pl.ds((c % 6) * CH, CH)], stage.at[slot], dsem.at[slot]
         )
 
+    def patch_copy(n):
+        return pltpu.make_async_copy((split, dual)[n], SD.at[pl.ds(n, 1)], isem.at[n])
+
     for c in range(NSTAGE):
         tile_copy(c, c).start()
+    for n in (0, 1):
+        patch_copy(n).start()
 
     def ag(rd, h, g, k):
         p, s = coord[g]
@@ -173,12 +176,22 @@
 
     def en(n, o):
         to = lax.rem(e + o, 8)
-        dst = T if n == 0 else MB
+        src = TP.at[n, to] if n < 3 else AS2.at[6]
         return pltpu.make_async_remote_copy(
-            src_ref=TP.at[n, to], dst_ref=dst.at[e],
+            src_ref=src, dst_ref=(T, MX, MD, MS)[n].at[e],
             send_sem=en_s.at[n, o], recv_sem=en_r.at[n, o],
             device_id={"energy": to}, device_id_type=pl.DeviceIdType.MESH,
         )
+
+    def en_volume(n, what):
+        for to in range(8):
+            for i in (0, 1):
+                blk = 2 * to + i
+                for h in (0, 1):
+                    TP[n, to, i, h] = what[h, blk // 8, blk % 8]
+        for o in range(1, 8):
+            en(n, o).start()
+        (T, MX, MD)[n][e] = TP[n, e]
 
     def own_rows(g):
         return pl.ds(g * 128, 8)
@@ -189,14 +202,18 @@
             X[h, blk // 8, blk % 8] = piece
         for g in (0, 1):
             V[0][h][own_rows(g)] = X[h, g]
+    pl.semaphore_wait(barrier, 13)
+    for h in (0, 1):
         ag_step(0, h, 0)
 
+    for n in (0, 1):
+        patch_copy(n).wait()
     for to in range(8):
         for i in (0, 1):
             for h in (0, 1):
                 cols = slice(i * 256 + h * 128, i * 256 + h * 128 + 128)
                 rows = slice(to * 8, to * 8 + 8)
-                TP[0, to, i, h] = split[0, rows, cols] - dual[0, rows, cols]
+                TP[0, to, i, h] = SD[0, rows, cols] - SD[1, rows, cols]
     T[e] = TP[0, e]
     for o in range(1, 8):
         en(0, o).start()
@@ -289,7 +306,6 @@
         fwd(rd, 0, 2, 4)
         ag_step(rd, 1, 2)
         fwd(rd, 1, 0, 4)
-        ag_sent(rd)
         if rd == 0:
             for b in range(4):
                 w = scale(b) * (sino[:, b * 128 : b * 128 + 128] - Pq[b])
@@ -330,6 +346,7 @@
             bwd(1, 2, 4)
             scatter(1)
             rs_step(rd, 1, 0)
+            ag_sent(rd)
             rs_step(rd, 0, 1)
             rs_step(rd, 1, 1)
             if rd > 0:
@@ -356,27 +373,26 @@
             ag_step(rd + 1, 0, 1)
             ag_step(rd + 1, 1, 1)
             rs_sent(rd)
+            if rd == 2:
+                en_volume(1, X)
         else:
+            en_volume(2, D)
+            ag_sent(rd)
             ar_mid(2 * rd - 1)
             alpha = rr / ar_end(2 * rd - 1)
+            AS2[6] = alpha
+            MS[e] = alpha
+            for o in range(1, 8):
+                en(3, o).start()
             for h in (0, 1):
-                for g in (0, 1):
-                    X[h, g] = X[h, g] + alpha * D[h, g]
-    for to in range(8):
-        for i in (0, 1):
-            for h in (0, 1):
-                blk = 2 * to + i
-                TP[1, to, i, h] = X[h, blk // 8, blk % 8]
-    for o in range(1, 8):
-        en(1, o).start()
-    MB[e] = TP[1, e]
-    for h in (0, 1):
-        for blk in range(16):
-            vol_out[:, blk * 256 + h * 128 : blk * 256 + h * 128 + 128] = X[h, blk // 8, blk % 8]
-    for o in range(1, 8):
-        en(1, o).wait_recv()
-    mb_out[...] = MB[...]
-    for n in (0, 1):
+                for blk in range(16):
+                    cols = slice(blk * 256 + h * 128, blk * 256 + h * 128 + 128)
+                    vol_out[:, cols] = X[h, blk // 8, blk % 8] + alpha * D[h, blk // 8, blk % 8]
+    for n in (1, 2, 3):
+        for o in range(1, 8):
+            en(n, o).wait_recv()
+        (mx_out, md_out, step_out)[n - 1][...] = (MX, MD, MS)[n - 1][...]
+    for n in range(4):
         for o in range(1, 8):
             en(n, o).wait_send()
 
@@ -388,14 +404,17 @@
     return a, b, (rest - b.astype(F32)).astype(BF16)
 
 
-def shrink_kernel(mb, dual, split_out, dual_out, M, B, GA, GB):
+def shrink_kernel(mx, md, step, dual, vol, vol_out, split_out, dual_out, M, B, GA, GB):
+    vol_out[...] = vol[...]
+    steps = step[...].reshape(64, 128)
     lane = lax.broadcasted_iota(jnp.int32, (64, 128), 1)
     row = lax.broadcasted_iota(jnp.int32, (64, 128), 0)
     left = lane < 64
     for i in (0, 1):
         for h in (0, 1):
             n = i * 2 + h
-            b = mb[:, i, h].reshape(64, 128) + dual[0, :, n * 128 : n * 128 + 128]
+            volume = mx[:, i, h].reshape(64, 128) + steps * md[:, i, h].reshape(64, 128)
+            b = volume + dual[0, :, n * 128 : n * 128 + 128]
             B[n] = b
             turned = pltpu.roll(b, 64, axis=1)
             for side in (0, 1):
@@ -471,14 +490,17 @@
     idx = jnp.concatenate([vrow, prev, final])
     vmem = pl.BlockSpec(memory_space=pltpu.VMEM)
     smem = pl.BlockSpec(memory_space=pltpu.SMEM)
-    volume, mb = pl.pallas_call(
+    anywhere = pl.BlockSpec(memory_space=pl.ANY)
+    volume, mx, md, step = pl.pallas_call(
         main_kernel,
         out_shape=(
             jax.ShapeDtypeStruct((8, 4096), F32),
             jax.ShapeDtypeStruct((8, 2, 2, 8, 128), F32),
+            jax.ShapeDtypeStruct((8, 2, 2, 8, 128), F32),
+            jax.ShapeDtypeStruct((8, 8, 128), F32),
         ),
-        in_specs=[smem, smem, pl.BlockSpec(memory_space=pl.ANY)] + [vmem] * 5,
-        out_specs=(vmem, vmem),
+        in_specs=[smem, smem, anywhere, vmem, vmem, vmem, anywhere, anywhere],
+        out_specs=(vmem,) * 4,
         scratch_shapes=[
             pltpu.VMEM((2, 4, 24, 256, 256), BF16),
             pltpu.VMEM((NSTAGE, CH, 128, 256), F32),
@@ -490,41 +512,45 @@
             pltpu.VMEM((2, 2, 8, 8, 128), F32),
             pltpu.VMEM((2, 2, 8, 8, 128), F32),
             pltpu.VMEM((8, 2, 2, 8, 128), F32),
-            pltpu.VMEM((2, 8, 2, 2, 8, 128), F32),
+            pltpu.VMEM((3, 8, 2, 2, 8, 128), F32),
             pltpu.VMEM((8, 2, 2, 8, 128), F32),
+            pltpu.VMEM((8, 2, 2, 8, 128), F32),
+            pltpu.VMEM((8, 8, 128), F32),
+            pltpu.VMEM((2, 64, 512), F32),
             pltpu.VMEM((4, 8, 128), F32),
             pltpu.VMEM((4, 8, 128), F32),
             pltpu.VMEM((4, 16, 256), BF16),
             pltpu.VMEM((6, 8, 128), F32),
-            pltpu.VMEM((6, 8, 128), F32),
+            pltpu.VMEM((7, 8, 128), F32),
             pltpu.VMEM((6, 6, 8, 128), F32),
             pltpu.SemaphoreType.DMA((NSTAGE,)),
+            pltpu.SemaphoreType.DMA((2,)),
             pltpu.SemaphoreType.DMA((4, 2, 2, 9)),
             pltpu.SemaphoreType.DMA((4, 2, 2, 9)),
             pltpu.SemaphoreType.DMA((3, 2, 2, 9)),
             pltpu.SemaphoreType.DMA((3, 2, 2, 9)),
             pltpu.SemaphoreType.DMA((6, 6)),
             pltpu.SemaphoreType.DMA((6, 6)),
-            pltpu.SemaphoreType.DMA((2, 8)),
-            pltpu.SemaphoreType.DMA((2, 8)),
+            pltpu.SemaphoreType.DMA((4, 8)),
+            pltpu.SemaphoreType.DMA((4, 8)),
         ],
         compiler_params=pltpu.CompilerParams(
             collective_id=0, has_side_effects=True, vmem_limit_bytes=56 * 1024 * 1024
         ),
         name="solve",
     )(idx, counts, tiles, sino, wts, x0, split, dual)
-    new_split, new_dual = pl.pallas_call(
+    volume, new_split, new_dual = pl.pallas_call(
         shrink_kernel,
-        out_shape=(jax.ShapeDtypeStruct((1, 64, 512), F32),) * 2,
-        in_specs=[vmem, vmem],
-        out_specs=(vmem, vmem),
+        out_shape=(jax.ShapeDtypeStruct((8, 4096), F32),) + (jax.ShapeDtypeStruct((1, 64, 512), F32),) * 2,
+        in_specs=[vmem] * 5,
+        out_specs=(vmem,) * 3,
         scratch_shapes=[
             pltpu.VMEM((8, 64, 128), F32), pltpu.VMEM((4, 64, 128), F32),
             pltpu.VMEM((8, 256, 256), BF16), pltpu.VMEM((8, 256, 128), BF16),
         ],
         compiler_params=pltpu.CompilerParams(vmem_limit_bytes=16 * 1024 * 1024),
         name="shrink",
-    )(mb, dual)
+    )(mx, md, step, dual, volume)
     return volume, new_split, new_dual
 
 

time: 172 us -> 172 us (level)
    unnamed x5 -> x10, local copies, waits for them, and re-layouts: 2.47 us -> 3.47 us
where the time goes in v3:
time: 172 us
  Pallas kernels  166 us (97%)
  local copies, waits for them, and re-layouts  4.27 us (2%)
    pallas_call x1, Pallas kernels, local(): pl.pallas_call(main_kernel, out_shape=(jax.ShapeDtypeStruct((8, 4096), F3...  157 us
    pallas_call x1, Pallas kernels, local(): pl.pallas_call(shrink_kernel, out_shape=(jax.ShapeDtypeStruct((8, 4096),...  8.76 us
    unnamed x10, local copies, waits for them, and re-layouts  3.47 us

profile of v3, /device:TPU:1, one launch (start us, length us, event | category | flops | bytes accessed | tf_op | source)
XLA Modules:
  0.0 171.9 jit_solution(14384551021411304191)
XLA Ops:
  0.6 0.0 copy-start
  0.7 0.8 reshape.139
  1.5 0.2 select_reduce_fusion.1
  1.7 0.1 select_reduce_fusion
  1.8 0.7 pad_add_fusion.idx
  2.5 157.2 %solve.1 = (f32[8,4096]{1,0:T(8,128)}, f32[8,2,2,8,128]{4,3,2,1,0:T(8,128)}, f32[8,2,2,8,128]{4,3,2,1,0:T(8,128)}, f32[8,8,128]{2,1,0:T(8,128)}) custom-call(s32[640]{0:T(1024)} %pad_add_fusion.idx, s32[4]{0:T(128)} %counts.1, f32[4,48,128,256]{3,2,1,0:T(8,128)} %tiles.1, f32[8,512]{1,0:T(8,128)} %sino.1, f32[8,512]{1,0:T(8,128)} %wts.1, f32[8,4096]{1,0:T(8,128)} %x0.1, ...), custom_call_target="tpu_custom_call" | custom-call | tf_op jit(solution)/shard_map/solve/pallas_call | solution.py:494
  159.7 0.0 copy-done
  159.7 0.0 copy-start.1
  159.7 0.9 copy-done.1
  160.6 0.0 copy-start.2
  160.6 0.9 copy-done.2
  161.5 0.0 copy-start.3
  161.5 0.9 copy-done.3
  162.4 0.0 copy-start.4
  162.4 0.8 copy-done.4
  163.1 8.8 %shrink.1 = (f32[8,4096]{1,0:T(8,128)}, f32[1,64,512]{2,1,0:T(8,128)}, f32[1,64,512]{2,1,0:T(8,128)}) custom-call(f32[8,2,2,8,128]{4,3,2,1,0:T(8,128)S(1)} %copy-done.2, f32[8,2,2,8,128]{4,3,2,1,0:T(8,128)S(1)} %copy-done.3, f32[8,8,128]{2,1,0:T(8,128)S(1)} %copy-done.4, f32[1,64,512]{2,1,0:T(8,128)S(1)} %copy-done, f32[8,4096]{1,0:T(8,128)S(1)} %copy-done.1), custom_call_target="tpu_custom_call" | custom-call | tf_op jit(solution)/shard_map/shrink/pallas_call | solution.py:542
  (1 shorter events, 0.0 us)
Async XLA Ops:
  0.6 159.0 %copy-start = (f32[1,64,512]{2,1,0:T(8,128)S(1)}, f32[1,64,512]{2,1,0:T(8,128)}, u32[]{:S(2)}) copy-start(f32[1,64,512]{2,1,0:T(8,128)} %dual.3) | copy-start | bytes 393220
  159.7 0.9 copy-start.1
  160.6 0.9 copy-start.2
  161.5 0.9 copy-start.3
  162.4 0.8 copy-start.4

commit v4 on v3

--- a/solution.py
+++ b/solution.py
@@ -30,8 +30,8 @@
     vol_out, mx_out, md_out, step_out,
     W, stage,
     V00, V01, V10, V11, V20, V21, V30, V31,
-    F, RB1, RB2, R, X, D, T, TP, MX, MD, MS, SD, Pq, Q, WL, AS, AS2, AR,
-    dsem, isem, ag_s, ag_r, rs_s, rs_r, ar_s, ar_r, en_s, en_r,
+    F, RB1, RB2, R, X, D, T, TP, MX, MD, MS, SD, XS, RS, VO, Pq, Q, WL, AS, AS2, AR,
+    dsem, isem, osem, ag_s, ag_r, rs_s, rs_r, ar_s, ar_r, en_s, en_r,
 ):
     V = ((V00, V01), (V10, V11), (V20, V21), (V30, V31))
     e = lax.axis_index("energy")
@@ -50,18 +50,24 @@
         pl.semaphore_signal(barrier, inc=1, device_id=at_views(0, x, y + o), device_id_type=pl.DeviceIdType.MESH)
     for o in range(1, 8):
         pl.semaphore_signal(barrier, inc=1, device_id={"energy": lax.rem(e + o, 8)}, device_id_type=pl.DeviceIdType.MESH)
+
     def tile_copy(c, slot):
         return pltpu.make_async_copy(
             tiles.at[c // 6, pl.ds((c % 6) * CH, CH)], stage.at[slot], dsem.at[slot]
         )
 
-    def patch_copy(n):
-        return pltpu.make_async_copy((split, dual)[n], SD.at[pl.ds(n, 1)], isem.at[n])
-
+    def read(n):
+        to = (SD.at[pl.ds(0, 1)], SD.at[pl.ds(1, 1)], XS, RS.at[0], RS.at[1])[n]
+        return pltpu.make_async_copy((split, dual, x0, sino, wts)[n], to, isem.at[n])
+
+    def write(n):
+        return pltpu.make_async_copy((MX, MD, MS, VO)[n], (mx_out, md_out, step_out, vol_out)[n], osem.at[n])
+
+
+    for n in (2, 0, 1, 3, 4):
+        read(n).start()
     for c in range(NSTAGE):
         tile_copy(c, c).start()
-    for n in (0, 1):
-        patch_copy(n).start()
 
     def ag(rd, h, g, k):
         p, s = coord[g]
@@ -73,8 +79,15 @@
         )[k // 3]
         return pltpu.make_async_remote_copy(
             src_ref=V[rd][h].at[pl.ds(base + src, size)], dst_ref=V[rd][h].at[pl.ds(base + dst, size)],
-            send_sem=ag_s.at[rd, h, g, k], recv_sem=ag_r.at[rd, h, g, k],
+            send_sem=ag_s.at[rd, h, g], recv_sem=ag_r.at[rd, h, g, min(k // 3, 1)],
             device_id=at_views(g, *dev), device_id_type=pl.DeviceIdType.MESH,
+        )
+
+    def ag_bytes(rd, h, g, size, k):
+        return pltpu.make_async_remote_copy(
+            src_ref=V[rd][h].at[pl.ds(0, size)], dst_ref=V[rd][h].at[pl.ds(0, size)],
+            send_sem=ag_s.at[rd, h, g], recv_sem=ag_r.at[rd, h, g, k],
+            device_id=at_views(g, coord[g][0] + 1, coord[g][1]), device_id_type=pl.DeviceIdType.MESH,
         )
 
     def ag_step(rd, h, n):
@@ -84,20 +97,17 @@
                     ag(rd, h, g, k).start()
         if n == 1:
             for g in (0, 1):
-                for k in (0, 1, 2):
-                    ag(rd, h, g, k).wait_recv()
+                ag_bytes(rd, h, g, 24, 0).wait_recv()
                 for k in (7, 6, 8):
                     ag(rd, h, g, k).start()
         if n == 2:
             for g in (0, 1):
-                for k in range(3, 9):
-                    ag(rd, h, g, k).wait_recv()
+                ag_bytes(rd, h, g, 96, 1).wait_recv()
 
     def ag_sent(rd):
         for h in (0, 1):
             for g in (0, 1):
-                for k in range(9):
-                    ag(rd, h, g, k).wait_send()
+                ag_bytes(rd, h, g, 120, 0).wait_send()
 
     def rs(rd, h, g, k):
         p, s = coord[g]
@@ -110,8 +120,15 @@
         land = RB1.at[rd, h, g, k] if k < 3 else RB2.at[rd, h, g, k - 3]
         return pltpu.make_async_remote_copy(
             src_ref=F.at[h, pl.ds(base + src, size)], dst_ref=land,
-            send_sem=rs_s.at[rd, h, g, k], recv_sem=rs_r.at[rd, h, g, k],
+            send_sem=rs_s.at[rd, h, g], recv_sem=rs_r.at[rd, h, g, min(k // 3, 1)],
             device_id=at_views(g, *dev), device_id_type=pl.DeviceIdType.MESH,
+        )
+
+    def rs_bytes(rd, h, g, size, k):
+        return pltpu.make_async_remote_copy(
+            src_ref=F.at[h, pl.ds(0, size)], dst_ref=F.at[h, pl.ds(0, size)],
+            send_sem=rs_s.at[rd, h, g], recv_sem=rs_r.at[rd, h, g, k],
+            device_id=at_views(g, coord[g][0] + 1, coord[g][1]), device_id_type=pl.DeviceIdType.MESH,
         )
 
     def rs_step(rd, h, n):
@@ -121,16 +138,14 @@
                     rs(rd, h, g, k).start()
         if n == 1:
             for g in (0, 1):
-                for k in (0, 1, 2):
-                    rs(rd, h, g, k).wait_recv()
+                rs_bytes(rd, h, g, 72, 0).wait_recv()
                 line = pl.ds(g * 128 + 8, 24)
                 F[h, line] = F[h, line] + RB1[rd, h, g, 0] + RB1[rd, h, g, 1] + RB1[rd, h, g, 2]
                 for k in (7, 6, 8):
                     rs(rd, h, g, k).start()
         if n == 2:
             for g in (0, 1):
-                for k in range(3, 9):
-                    rs(rd, h, g, k).wait_recv()
+                rs_bytes(rd, h, g, 48, 1).wait_recv()
 
     def rs_total(rd, h, g):
         total = F[h, own_rows(g)]
@@ -141,8 +156,7 @@
     def rs_sent(rd):
         for h in (0, 1):
             for g in (0, 1):
-                for k in range(9):
-                    rs(rd, h, g, k).wait_send()
+                rs_bytes(rd, h, g, 120, 0).wait_send()
 
     def ar(n, k):
         src = AS if k < 3 else AS2
@@ -196,9 +210,10 @@
     def own_rows(g):
         return pl.ds(g * 128, 8)
 
+    read(2).wait()
     for h in (0, 1):
         for blk in range(16):
-            piece = x0[:, blk * 256 + h * 128 : blk * 256 + h * 128 + 128]
+            piece = XS[:, blk * 256 + h * 128 : blk * 256 + h * 128 + 128]
             X[h, blk // 8, blk % 8] = piece
         for g in (0, 1):
             V[0][h][own_rows(g)] = X[h, g]
@@ -206,8 +221,8 @@
     for h in (0, 1):
         ag_step(0, h, 0)
 
-    for n in (0, 1):
-        patch_copy(n).wait()
+    for n in (0, 1, 3, 4):
+        read(n).wait()
     for to in range(8):
         for i in (0, 1):
             for h in (0, 1):
@@ -228,9 +243,12 @@
             jp = (c % 6) * (CH // 2) + u
             for h in (0, 1):
                 for t in (0, 1):
-                    hi, lo = split2(stage[slot, 2 * u + t, :, h * 128 : h * 128 + 128])
-                    W[h, b, jp, 0:128, t * 128 : t * 128 + 128] = hi
-                    W[h, b, jp, 128:256, t * 128 : t * 128 + 128] = lo
+                    part = stage[slot, 2 * u + t, :, h * 128 : h * 128 + 128]
+                    here = slice(t * 128, t * 128 + 128)
+                    if h == 0:
+                        W[h, b, jp, 0:128, here], W[h, b, jp, 128:256, here] = split2(part)
+                    else:
+                        W[h, b, jp, here, 0:128], W[h, b, jp, here, 128:256] = split2(part.T)
 
         @pl.when(c + NSTAGE < 24)
         def _():
@@ -248,7 +266,7 @@
                 hi, lo = split2(jnp.concatenate([v0, v1], axis=1))
                 acc = acc + lax.dot_general(
                     jnp.concatenate([hi, lo], axis=0), W[h, b, jp],
-                    (((1,), (1,)), ((), ())), preferred_element_type=F32,
+                    (((1,), (1 - h,)), ((), ())), preferred_element_type=F32,
                 )
             both = acc[0:8] + acc[8:16]
             part = both[:, 0:128] + both[:, 128:256]
@@ -266,7 +284,7 @@
             for jp in range(24):
                 i = b * 48 + 2 * jp
                 out = lax.dot_general(
-                    lhs, W[h, b, jp], (((1,), (0,)), ((), ())), preferred_element_type=F32
+                    lhs, W[h, b, jp], (((1,), (h,)), ((), ())), preferred_element_type=F32
                 )
                 both = out[0:8] + out[8:16]
                 R[i + 1] = both[:, 0:128] + R[idx[192 + i]]
@@ -286,7 +304,7 @@
     lane = lax.broadcasted_iota(jnp.int32, (8, 128), 1)
 
     def scale(b):
-        return jnp.where(lane < counts[b], wts[:, b * 128 : b * 128 + 128], 0.0)
+        return jnp.where(lane < counts[b], RS[1, :, b * 128 : b * 128 + 128], 0.0)
 
     def squares(v):
         return jnp.sum(v * v, axis=0)
@@ -308,7 +326,7 @@
         fwd(rd, 1, 0, 4)
         if rd == 0:
             for b in range(4):
-                w = scale(b) * (sino[:, b * 128 : b * 128 + 128] - Pq[b])
+                w = scale(b) * (RS[0, :, b * 128 : b * 128 + 128] - Pq[b])
                 hi, lo = split2(w)
                 WL[b] = jnp.concatenate(
                     [jnp.concatenate([hi, hi], axis=1), jnp.concatenate([lo, lo], axis=1)], axis=0
@@ -387,14 +405,17 @@
             for h in (0, 1):
                 for blk in range(16):
                     cols = slice(blk * 256 + h * 128, blk * 256 + h * 128 + 128)
-                    vol_out[:, cols] = X[h, blk // 8, blk % 8] + alpha * D[h, blk // 8, blk % 8]
+                    VO[:, cols] = X[h, blk // 8, blk % 8] + alpha * D[h, blk // 8, blk % 8]
+    write(3).start()
     for n in (1, 2, 3):
         for o in range(1, 8):
             en(n, o).wait_recv()
-        (mx_out, md_out, step_out)[n - 1][...] = (MX, MD, MS)[n - 1][...]
+        write(n - 1).start()
     for n in range(4):
         for o in range(1, 8):
             en(n, o).wait_send()
+    for n in range(4):
+        write(n).wait()
 
 
 def split3(v):
@@ -404,8 +425,22 @@
     return a, b, (rest - b.astype(F32)).astype(BF16)
 
 
-def shrink_kernel(mx, md, step, dual, vol, vol_out, split_out, dual_out, M, B, GA, GB):
-    vol_out[...] = vol[...]
+def shrink_kernel(
+    mx_in, md_in, step_in, dual_in, vol, vol_out, split_out, dual_out,
+    mx, md, step, dual, SO, DO, M, B, GA, GB, isem, osem,
+):
+    passed = pltpu.make_async_copy(vol, vol_out, isem.at[4])
+    passed.start()
+    reads = [
+        pltpu.make_async_copy(a, b, isem.at[n])
+        for n, (a, b) in enumerate(((mx_in, mx), (md_in, md), (step_in, step), (dual_in, dual)))
+    ]
+    for one in reads:
+        one.start()
+    GA[...] = jnp.zeros_like(GA)
+    GB[...] = jnp.zeros_like(GB)
+    for one in reads:
+        one.wait()
     steps = step[...].reshape(64, 128)
     lane = lax.broadcasted_iota(jnp.int32, (64, 128), 1)
     row = lax.broadcasted_iota(jnp.int32, (64, 128), 0)
@@ -429,8 +464,6 @@
     place = lax.broadcasted_iota(jnp.int32, (8, 128), 0)
     none = jnp.zeros((8, 128), F32)
     blank = jnp.zeros((16, 128), BF16)
-    GA[...] = jnp.zeros_like(GA)
-    GB[...] = jnp.zeros_like(GB)
     for kb in range(8):
         heads = [M[p, kb * 8 : kb * 8 + 8, :] for p in range(8)]
         for j in range(8):
@@ -469,8 +502,14 @@
             b = B[n]
             cols = slice(n * 128, n * 128 + 128)
             new_split = b - SHRINK * solved
-            split_out[0, :, cols] = new_split
-            dual_out[0, :, cols] = b - new_split
+            SO[0, :, cols] = new_split
+            DO[0, :, cols] = b - new_split
+    writes = [pltpu.make_async_copy(SO, split_out, osem.at[0]), pltpu.make_async_copy(DO, dual_out, osem.at[1])]
+    for one in writes:
+        one.start()
+    for one in writes:
+        one.wait()
+    passed.wait()
 
 
 def local(tiles, tile_blocks, counts, sino, wts, x0, split, dual):
@@ -488,7 +527,6 @@
     rows = jnp.arange(256, dtype=jnp.int32)
     final = jnp.max(jnp.where(rows[:, None] == vrow[None, :], order[None, :] + 1, 0), axis=1)
     idx = jnp.concatenate([vrow, prev, final])
-    vmem = pl.BlockSpec(memory_space=pltpu.VMEM)
     smem = pl.BlockSpec(memory_space=pltpu.SMEM)
     anywhere = pl.BlockSpec(memory_space=pl.ANY)
     volume, mx, md, step = pl.pallas_call(
@@ -499,8 +537,8 @@
             jax.ShapeDtypeStruct((8, 2, 2, 8, 128), F32),
             jax.ShapeDtypeStruct((8, 8, 128), F32),
         ),
-        in_specs=[smem, smem, anywhere, vmem, vmem, vmem, anywhere, anywhere],
-        out_specs=(vmem,) * 4,
+        in_specs=[smem, smem] + [anywhere] * 6,
+        out_specs=(anywhere,) * 4,
         scratch_shapes=[
             pltpu.VMEM((2, 4, 24, 256, 256), BF16),
             pltpu.VMEM((NSTAGE, CH, 128, 256), F32),
@@ -517,6 +555,9 @@
             pltpu.VMEM((8, 2, 2, 8, 128), F32),
             pltpu.VMEM((8, 8, 128), F32),
             pltpu.VMEM((2, 64, 512), F32),
+            pltpu.VMEM((8, 4096), F32),
+            pltpu.VMEM((2, 8, 512), F32),
+            pltpu.VMEM((8, 4096), F32),
             pltpu.VMEM((4, 8, 128), F32),
             pltpu.VMEM((4, 8, 128), F32),
             pltpu.VMEM((4, 16, 256), BF16),
@@ -524,11 +565,12 @@
             pltpu.VMEM((7, 8, 128), F32),
             pltpu.VMEM((6, 6, 8, 128), F32),
             pltpu.SemaphoreType.DMA((NSTAGE,)),
-            pltpu.SemaphoreType.DMA((2,)),
-            pltpu.SemaphoreType.DMA((4, 2, 2, 9)),
-            pltpu.SemaphoreType.DMA((4, 2, 2, 9)),
-            pltpu.SemaphoreType.DMA((3, 2, 2, 9)),
-            pltpu.SemaphoreType.DMA((3, 2, 2, 9)),
+            pltpu.SemaphoreType.DMA((5,)),
+            pltpu.SemaphoreType.DMA((4,)),
+            pltpu.SemaphoreType.DMA((4, 2, 2)),
+            pltpu.SemaphoreType.DMA((4, 2, 2, 2)),
+            pltpu.SemaphoreType.DMA((3, 2, 2)),
+            pltpu.SemaphoreType.DMA((3, 2, 2, 2)),
             pltpu.SemaphoreType.DMA((6, 6)),
             pltpu.SemaphoreType.DMA((6, 6)),
             pltpu.SemaphoreType.DMA((4, 8)),
@@ -542,13 +584,17 @@
     volume, new_split, new_dual = pl.pallas_call(
         shrink_kernel,
         out_shape=(jax.ShapeDtypeStruct((8, 4096), F32),) + (jax.ShapeDtypeStruct((1, 64, 512), F32),) * 2,
-        in_specs=[vmem] * 5,
-        out_specs=(vmem,) * 3,
+        in_specs=[anywhere] * 5,
+        out_specs=(anywhere,) * 3,
         scratch_shapes=[
+            pltpu.VMEM((8, 2, 2, 8, 128), F32), pltpu.VMEM((8, 2, 2, 8, 128), F32),
+            pltpu.VMEM((8, 8, 128), F32), pltpu.VMEM((1, 64, 512), F32),
+            pltpu.VMEM((1, 64, 512), F32), pltpu.VMEM((1, 64, 512), F32),
             pltpu.VMEM((8, 64, 128), F32), pltpu.VMEM((4, 64, 128), F32),
             pltpu.VMEM((8, 256, 256), BF16), pltpu.VMEM((8, 256, 128), BF16),
+            pltpu.SemaphoreType.DMA((5,)), pltpu.SemaphoreType.DMA((2,)),
         ],
-        compiler_params=pltpu.CompilerParams(vmem_limit_bytes=16 * 1024 * 1024),
+        compiler_params=pltpu.CompilerParams(vmem_limit_bytes=60 * 1024 * 1024),
         name="shrink",
     )(mx, md, step, dual, volume)
     return volume, new_split, new_dual

time: 172 us -> 161 us (0.936)
  Pallas kernels: 166 us -> 158 us
  local copies, waits for them, and re-layouts: 4.27 us -> 0.76 us
    pallas_call x1, Pallas kernels: 157 us -> 149 us  [local(): pl.pallas_call(main_kernel, out_shape=(jax.ShapeDtypeStruct((8, 4096), F3...]
    unnamed x10 -> x0, local copies, waits for them, and re-layouts: 3.47 us -> none
where the time goes in v4:
time: 161 us
  Pallas kernels  158 us (98%)
    pallas_call x1, Pallas kernels, local(): pl.pallas_call(main_kernel, out_shape=(jax.ShapeDtypeStruct((8, 4096), F3...  149 us
    pallas_call x1, Pallas kernels, local(): pl.pallas_call(shrink_kernel, out_shape=(jax.ShapeDtypeStruct((8, 4096),...  9.86 us

profile of v4, /device:TPU:1, one launch (start us, length us, event | category | flops | bytes accessed | tf_op | source)
XLA Modules:
  0.0 161.0 jit_solution(16538117879454732268)
XLA Ops:
  0.6 0.8 reshape.139
  1.4 0.2 select_reduce_fusion.1
  1.6 0.1 select_reduce_fusion
  1.8 0.7 pad_add_fusion.idx
  2.4 148.5 %solve.1 = (f32[8,4096]{1,0:T(8,128)}, f32[8,2,2,8,128]{4,3,2,1,0:T(8,128)}, f32[8,2,2,8,128]{4,3,2,1,0:T(8,128)}, f32[8,8,128]{2,1,0:T(8,128)}) custom-call(s32[640]{0:T(1024)} %pad_add_fusion.idx, s32[4]{0:T(128)} %counts.1, f32[4,48,128,256]{3,2,1,0:T(8,128)} %tiles.1, f32[8,512]{1,0:T(8,128)} %sino.1, f32[8,512]{1,0:T(8,128)} %wts.1, f32[8,4096]{1,0:T(8,128)} %x0.1, ...), custom_call_target="tpu_custom_call" | custom-call | tf_op jit(solution)/shard_map/solve/pallas_call | solution.py:532
  151.0 9.9 %shrink.1 = (f32[8,4096]{1,0:T(8,128)}, f32[1,64,512]{2,1,0:T(8,128)}, f32[1,64,512]{2,1,0:T(8,128)}) custom-call(f32[8,2,2,8,128]{4,3,2,1,0:T(8,128)} %get-tuple-element.7.mx_in, f32[8,2,2,8,128]{4,3,2,1,0:T(8,128)} %get-tuple-element.8.md_in, f32[8,8,128]{2,1,0:T(8,128)} %get-tuple-element.9.step_in, f32[1,64,512]{2,1,0:T(8,128)} %dual_in.1, ...), custom_call_target="tpu_custom_call" | custom-call | tf_op jit(solution)/shard_map/shrink/pallas_call | solution.py:584
  (1 shorter events, 0.0 us)

commit v5 on v4

--- a/solution.py
+++ b/solution.py
@@ -30,8 +30,8 @@
     vol_out, mx_out, md_out, step_out,
     W, stage,
     V00, V01, V10, V11, V20, V21, V30, V31,
-    F, RB1, RB2, R, X, D, T, TP, MX, MD, MS, SD, XS, RS, VO, Pq, Q, WL, AS, AS2, AR,
-    dsem, isem, osem, ag_s, ag_r, rs_s, rs_r, ar_s, ar_r, en_s, en_r,
+    F, RB1, RB2, R, X, D, T, TP, MX, MD, MS, SD, XS, RS, VO, Pq, Q, WL, AS, AS2, AR, AL,
+    dsem, isem, osem, ag_s, ag_r, rs_s, rs_r, ar_s, ar_r, al_s, al_r, en_s, en_r,
 ):
     V = ((V00, V01), (V10, V11), (V20, V21), (V30, V31))
     e = lax.axis_index("energy")
@@ -45,9 +45,8 @@
     coord = ((x, y), (y, x))
 
     barrier = pltpu.get_barrier_semaphore()
-    for o in (1, 2, 3):
-        pl.semaphore_signal(barrier, inc=1, device_id=at_views(0, x + o, y), device_id_type=pl.DeviceIdType.MESH)
-        pl.semaphore_signal(barrier, inc=1, device_id=at_views(0, x, y + o), device_id_type=pl.DeviceIdType.MESH)
+    for o in range(1, 16):
+        pl.semaphore_signal(barrier, inc=1, device_id={"views": lax.rem(a + o, 16)}, device_id_type=pl.DeviceIdType.MESH)
     for o in range(1, 8):
         pl.semaphore_signal(barrier, inc=1, device_id={"energy": lax.rem(e + o, 8)}, device_id_type=pl.DeviceIdType.MESH)
 
@@ -92,13 +91,13 @@
 
     def ag_step(rd, h, n):
         if n == 0:
-            for k in (1, 0, 2, 4, 3, 5):
+            for k in (0, 2, 1, 3, 5, 4):
                 for g in (0, 1):
                     ag(rd, h, g, k).start()
         if n == 1:
             for g in (0, 1):
                 ag_bytes(rd, h, g, 24, 0).wait_recv()
-                for k in (7, 6, 8):
+                for k in (6, 8, 7):
                     ag(rd, h, g, k).start()
         if n == 2:
             for g in (0, 1):
@@ -133,7 +132,7 @@
 
     def rs_step(rd, h, n):
         if n == 0:
-            for k in (1, 0, 2, 4, 3, 5):
+            for k in (0, 2, 1, 3, 5, 4):
                 for g in (0, 1):
                     rs(rd, h, g, k).start()
         if n == 1:
@@ -141,7 +140,7 @@
                 rs_bytes(rd, h, g, 72, 0).wait_recv()
                 line = pl.ds(g * 128 + 8, 24)
                 F[h, line] = F[h, line] + RB1[rd, h, g, 0] + RB1[rd, h, g, 1] + RB1[rd, h, g, 2]
-                for k in (7, 6, 8):
+                for k in (6, 8, 7):
                     rs(rd, h, g, k).start()
         if n == 2:
             for g in (0, 1):
@@ -164,8 +163,15 @@
         dev = at_views(0, x + o, y) if k < 3 else at_views(0, x, y + o)
         return pltpu.make_async_remote_copy(
             src_ref=src.at[n], dst_ref=AR.at[n, k],
-            send_sem=ar_s.at[n, k], recv_sem=ar_r.at[n, k],
+            send_sem=ar_s.at[n], recv_sem=ar_r.at[n, k // 3],
             device_id=dev, device_id_type=pl.DeviceIdType.MESH,
+        )
+
+    def ar_bytes(n, size, k):
+        return pltpu.make_async_remote_copy(
+            src_ref=AR.at[n, pl.ds(0, size)], dst_ref=AR.at[n, pl.ds(0, size)],
+            send_sem=ar_s.at[n], recv_sem=ar_r.at[n, k],
+            device_id=at_views(0, x + 1, y), device_id_type=pl.DeviceIdType.MESH,
         )
 
     def ar_start(n, value):
@@ -174,27 +180,44 @@
             ar(n, k).start()
 
     def ar_mid(n):
-        for k in range(3):
-            ar(n, k).wait_recv()
+        ar_bytes(n, 3, 0).wait_recv()
         AS2[n] = AS[n] + AR[n, 0] + AR[n, 1] + AR[n, 2]
         for k in range(3, 6):
             ar(n, k).start()
 
     def ar_end(n):
-        for k in range(3, 6):
-            ar(n, k).wait_recv()
+        ar_bytes(n, 3, 1).wait_recv()
         total = AS2[n] + AR[n, 3] + AR[n, 4] + AR[n, 5]
-        for k in range(6):
-            ar(n, k).wait_send()
+        ar_bytes(n, 6, 0).wait_send()
         return lane_total(total)
+
+    def last_sum(o):
+        return pltpu.make_async_remote_copy(
+            src_ref=AS.at[5], dst_ref=AL.at[o - 1], send_sem=al_s, recv_sem=al_r,
+            device_id={"views": lax.rem(a + o, 16)}, device_id_type=pl.DeviceIdType.MESH,
+        )
+
+    def last_bytes():
+        ref = AL.at[pl.ds(0, 15)]
+        return pltpu.make_async_remote_copy(
+            src_ref=ref, dst_ref=ref, send_sem=al_s, recv_sem=al_r,
+            device_id={"views": lax.rem(a + 1, 16)}, device_id_type=pl.DeviceIdType.MESH,
+        )
 
     def en(n, o):
         to = lax.rem(e + o, 8)
         src = TP.at[n, to] if n < 3 else AS2.at[6]
         return pltpu.make_async_remote_copy(
             src_ref=src, dst_ref=(T, MX, MD, MS)[n].at[e],
-            send_sem=en_s.at[n, o], recv_sem=en_r.at[n, o],
+            send_sem=en_s.at[n], recv_sem=en_r.at[n],
             device_id={"energy": to}, device_id_type=pl.DeviceIdType.MESH,
+        )
+
+    def en_bytes(n):
+        ref = (T, MX, MD, MS)[n].at[pl.ds(0, 7)]
+        return pltpu.make_async_remote_copy(
+            src_ref=ref, dst_ref=ref, send_sem=en_s.at[n], recv_sem=en_r.at[n],
+            device_id={"energy": lax.rem(e + 1, 8)}, device_id_type=pl.DeviceIdType.MESH,
         )
 
     def en_volume(n, what):
@@ -217,7 +240,7 @@
             X[h, blk // 8, blk % 8] = piece
         for g in (0, 1):
             V[0][h][own_rows(g)] = X[h, g]
-    pl.semaphore_wait(barrier, 13)
+    pl.semaphore_wait(barrier, 22)
     for h in (0, 1):
         ag_step(0, h, 0)
 
@@ -353,7 +376,12 @@
                     WL[b] = jnp.concatenate(
                         [jnp.concatenate([hi, hi], axis=1), jnp.concatenate([lo, lo], axis=1)], axis=0
                     )
-            ar_start(2 * rd - 1, curv)
+            if last:
+                AS[5] = curv
+                for o in (10, 6, 9, 11, 5, 7, 2, 8, 14, 3, 13, 1, 4, 12, 15):
+                    last_sum(o).start()
+            else:
+                ar_start(2 * rd - 1, curv)
         if not last:
             bwd(0, 0, 4)
             scatter(0)
@@ -370,12 +398,11 @@
             if rd > 0:
                 alpha = rr / ar_end(2 * rd - 1)
             else:
-                for o in range(1, 8):
-                    en(0, o).wait_recv()
+                en_bytes(0).wait_recv()
             norm = jnp.zeros((8, 128), F32)
             for h in (0, 1):
-                rs_step(rd, h, 2)
                 for g in (0, 1):
+                    rs_bytes(rd, h, g, 48, 1).wait_recv()
                     summed = rs_total(rd, h, g)
                     if rd == 0:
                         anchor = T[g * 4 : g * 4 + 4, :, h].reshape(8, 8, 128)
@@ -386,7 +413,8 @@
                         X[h, g] = X[h, g] + alpha * d_own
                     V[rd + 1][h][own_rows(g)] = r_own
                     norm = norm + squares(r_own)
-                ag_step(rd + 1, h, 0)
+                    for k in (0, 2, 1, 3, 5, 4):
+                        ag(rd + 1, h, g, k).start()
             ar_start(2 * rd, norm)
             ag_step(rd + 1, 0, 1)
             ag_step(rd + 1, 1, 1)
@@ -396,8 +424,11 @@
         else:
             en_volume(2, D)
             ag_sent(rd)
-            ar_mid(2 * rd - 1)
-            alpha = rr / ar_end(2 * rd - 1)
+            last_bytes().wait_recv()
+            total = AS[5]
+            for o in range(15):
+                total = total + AL[o]
+            alpha = rr / lane_total(total)
             AS2[6] = alpha
             MS[e] = alpha
             for o in range(1, 8):
@@ -408,12 +439,11 @@
                     VO[:, cols] = X[h, blk // 8, blk % 8] + alpha * D[h, blk // 8, blk % 8]
     write(3).start()
     for n in (1, 2, 3):
-        for o in range(1, 8):
-            en(n, o).wait_recv()
+        en_bytes(n).wait_recv()
         write(n - 1).start()
     for n in range(4):
-        for o in range(1, 8):
-            en(n, o).wait_send()
+        en_bytes(n).wait_send()
+    last_bytes().wait_send()
     for n in range(4):
         write(n).wait()
 
@@ -564,6 +594,7 @@
             pltpu.VMEM((6, 8, 128), F32),
             pltpu.VMEM((7, 8, 128), F32),
             pltpu.VMEM((6, 6, 8, 128), F32),
+            pltpu.VMEM((15, 8, 128), F32),
             pltpu.SemaphoreType.DMA((NSTAGE,)),
             pltpu.SemaphoreType.DMA((5,)),
             pltpu.SemaphoreType.DMA((4,)),
@@ -571,10 +602,12 @@
             pltpu.SemaphoreType.DMA((4, 2, 2, 2)),
             pltpu.SemaphoreType.DMA((3, 2, 2)),
             pltpu.SemaphoreType.DMA((3, 2, 2, 2)),
-            pltpu.SemaphoreType.DMA((6, 6)),
-            pltpu.SemaphoreType.DMA((6, 6)),
-            pltpu.SemaphoreType.DMA((4, 8)),
-            pltpu.SemaphoreType.DMA((4, 8)),
+            pltpu.SemaphoreType.DMA((6,)),
+            pltpu.SemaphoreType.DMA((6, 2)),
+            pltpu.SemaphoreType.DMA,
+            pltpu.SemaphoreType.DMA,
+            pltpu.SemaphoreType.DMA((4,)),
+            pltpu.SemaphoreType.DMA((4,)),
         ],
         compiler_params=pltpu.CompilerParams(
             collective_id=0, has_side_effects=True, vmem_limit_bytes=56 * 1024 * 1024

time: 161 us -> 159 us (0.988)
  Pallas kernels: 158 us -> 156 us
    pallas_call x1, Pallas kernels: 149 us -> 147 us  [local(): pl.pallas_call(main_kernel, out_shape=(jax.ShapeDtypeStruct((8, 4096), F3...]
where the time goes in v5:
time: 159 us
  Pallas kernels  156 us (98%)
    pallas_call x1, Pallas kernels, local(): pl.pallas_call(main_kernel, out_shape=(jax.ShapeDtypeStruct((8, 4096), F3...  147 us
    pallas_call x1, Pallas kernels, local(): pl.pallas_call(shrink_kernel, out_shape=(jax.ShapeDtypeStruct((8, 4096),...  9.86 us

profile of v5, /device:TPU:1, one launch (start us, length us, event | category | flops | bytes accessed | tf_op | source)
XLA Modules:
  0.0 159.0 jit_solution(6064244068551761906)
XLA Ops:
  0.6 0.8 reshape.139
  1.4 0.2 select_reduce_fusion.1
  1.6 0.1 select_reduce_fusion
  1.8 0.7 pad_add_fusion.idx
  2.4 146.6 %solve.1 = (f32[8,4096]{1,0:T(8,128)}, f32[8,2,2,8,128]{4,3,2,1,0:T(8,128)}, f32[8,2,2,8,128]{4,3,2,1,0:T(8,128)}, f32[8,8,128]{2,1,0:T(8,128)}) custom-call(s32[640]{0:T(1024)} %pad_add_fusion.idx, s32[4]{0:T(128)} %counts.1, f32[4,48,128,256]{3,2,1,0:T(8,128)} %tiles.1, f32[8,512]{1,0:T(8,128)} %sino.1, f32[8,512]{1,0:T(8,128)} %wts.1, f32[8,4096]{1,0:T(8,128)} %x0.1, ...), custom_call_target="tpu_custom_call" | custom-call | tf_op jit(solution)/shard_map/solve/pallas_call | solution.py:562
  149.0 9.9 %shrink.1 = (f32[8,4096]{1,0:T(8,128)}, f32[1,64,512]{2,1,0:T(8,128)}, f32[1,64,512]{2,1,0:T(8,128)}) custom-call(f32[8,2,2,8,128]{4,3,2,1,0:T(8,128)} %get-tuple-element.7.mx_in, f32[8,2,2,8,128]{4,3,2,1,0:T(8,128)} %get-tuple-element.8.md_in, f32[8,8,128]{2,1,0:T(8,128)} %get-tuple-element.9.step_in, f32[1,64,512]{2,1,0:T(8,128)} %dual_in.1, ...), custom_call_target="tpu_custom_call" | custom-call | tf_op jit(solution)/shard_map/shrink/pallas_call | solution.py:617
  (1 shorter events, 0.0 us)
